TPU v7x, 512 devices: a whole 4x4x16 slice. The times are simulated.
512 devices in a mesh: src: 8 (over x, y_lo), feat: 64 (over y_hi, z, core).
Axes of the slice: x: 4, y: 4 (y_hi: 2, y_lo: 2; y = y_hi * 2 + y_lo), z: 16, core: 2. Of those that a mesh axis runs over, the one named last changes fastest.
Arguments:
- residual: bfloat16 [448, 2304], P(None, 'src'), may hold values from -80 to 80
- token_ids: int32 [448], replicated, may hold values from 0 to 255999, as said below
- ffn_gain: bfloat16 [2304], P('src'), may hold values from 0.25 to 1.75
- gate_w: bfloat16 [2304, 18432], P('src', 'feat'), may hold values from -0.125 to 0.125
- up_w: bfloat16 [2304, 18432], P('src', 'feat'), may hold values from -0.125 to 0.125
- down_w: bfloat16 [18432, 2304], P('feat', 'src'), may hold values from -0.046875 to 0.046875
- enc_w: bfloat16 [2304, 65536], P(None, ('src', 'feat')), may hold values from -0.41666667 to 0.41666667
- enc_bias: bfloat16 [65536], P(('src', 'feat')), may hold values from -1 to 0.5
- dec_w: bfloat16 [65536, 2304], P(('src', 'feat')), may hold values from -0.0390625 to 0.0390625
- dec_bias: bfloat16 [2304], replicated, may hold values from -3 to 3
- enc_first: bfloat16 [2304, 65536], P(None, ('src', 'feat')), may hold values from -0.00010347366 to 0.00010347366
- enc_second: bfloat16 [2304, 65536], P(None, ('src', 'feat')), may hold values from 3.3105607e-10 to 3.3032848e-09
- dec_first: bfloat16 [65536, 2304], P(('src', 'feat')), may hold values from -0.00010347366 to 0.00010347366
- dec_second: bfloat16 [65536, 2304], P(('src', 'feat')), may hold values from 3.3105607e-10 to 3.3032848e-09
Outputs:
- enc_update: bfloat16 [2304, 65536], P(None, ('src', 'feat'))
- dec_update: bfloat16 [65536, 2304], P(('src', 'feat'))
Inputs may be any that keep to these rules, and one draw needn't show every extreme that they name: `token_ids`: token ids of the batch; ids under 4 are control tokens.
All inputs are finite; a program needn't handle non-finite values.
Results may differ from a plain program's by a relative error of at most 0.01.
Values may be sent and summed in bfloat16 or wider, within the bound.
A program may use at most 128 MiB of HBM per device.

v0:
```python
import jax
import jax.numpy as jnp
from jax import lax
from jax.sharding import PartitionSpec as P

SPECIAL = 4


eps_rms = 1e-06
beta_one = 0.9
beta_two = 0.999
adam_count = 100.0
l1_coeff = 0.2


def adam_direction(grad, first, second, clip_factor):
    scaled_grad = clip_factor * grad
    first_new = beta_one * first.astype(jnp.float32) + (1.0 - beta_one) * scaled_grad
    second_new = (
        beta_two * second.astype(jnp.float32) + (1.0 - beta_two) * scaled_grad * scaled_grad
    )
    corr_one = 1.0 - beta_one**adam_count
    corr_two = 1.0 - beta_two**adam_count
    return (first_new / corr_one / (jnp.sqrt(second_new / corr_two) + 1e-08)).astype(jnp.bfloat16)


def local(
    residual,
    token_ids,
    ffn_gain,
    gate_w,
    up_w,
    down_w,
    enc_w,
    enc_bias,
    dec_w,
    dec_bias,
    enc_first,
    enc_second,
    dec_first,
    dec_second,
):
    src_count = lax.axis_size("src")
    col_width = residual.shape[1]
    model_width = col_width * src_count
    res_float = residual.astype(jnp.float32)
    row_squares = lax.psum(jnp.sum(res_float * res_float, axis=1), "src")
    inverse_rms = lax.rsqrt(row_squares / model_width + eps_rms)
    normed = (res_float * inverse_rms[:, None] * ffn_gain.astype(jnp.float32)).astype(jnp.bfloat16)
    gate_part = jnp.dot(normed, gate_w, preferred_element_type=jnp.float32)
    up_part = jnp.dot(normed, up_w, preferred_element_type=jnp.float32)
    gate_acts, up_acts = lax.psum((gate_part, up_part), "src")
    hidden = (jax.nn.gelu(gate_acts, approximate=True) * up_acts).astype(jnp.bfloat16)
    out_part = jnp.dot(hidden, down_w, preferred_element_type=jnp.float32)
    ffn_out = lax.psum(out_part, "feat")
    stream = (res_float + ffn_out).astype(jnp.bfloat16)
    stream_float = stream.astype(jnp.float32)
    stream_squares = lax.psum(jnp.sum(stream_float * stream_float, axis=1), "src")
    scaled_part = (
        stream_float * lax.rsqrt(stream_squares / model_width + eps_rms)[:, None]
    ).astype(jnp.bfloat16)
    scaled = lax.all_gather(scaled_part, "src", axis=1, tiled=True)
    pre_acts = jnp.dot(scaled, enc_w, preferred_element_type=jnp.float32) + enc_bias.astype(
        jnp.float32
    )
    latents = jnp.maximum(pre_acts, 0.0).astype(jnp.bfloat16)
    recon_terms = jnp.dot(latents, dec_w, preferred_element_type=jnp.float32)
    target = scaled.astype(jnp.float32) - dec_bias.astype(jnp.float32)[None, :]
    row_share = lax.psum_scatter(recon_terms, "feat", scatter_dimension=0, tiled=True)
    share_block = lax.psum_scatter(row_share, "src", scatter_dimension=1, tiled=True)
    row_start = lax.axis_index("feat") * share_block.shape[0]
    col_start = lax.axis_index("src") * share_block.shape[1]
    target_block = lax.dynamic_slice(target, (row_start, col_start), share_block.shape)
    err_block = (share_block - target_block).astype(jnp.bfloat16)
    err_cols = lax.all_gather(err_block, "src", axis=1, tiled=True)
    errors = lax.all_gather(err_cols, "feat", axis=0, tiled=True)
    live_mask = (token_ids >= SPECIAL).astype(jnp.float32)
    token_weight = live_mask / jnp.maximum(jnp.sum(live_mask), 1.0)
    err_grad = (2.0 * token_weight[:, None] * errors.astype(jnp.float32)).astype(jnp.bfloat16)
    dec_grad = jnp.einsum("tf,td->fd", latents, err_grad, preferred_element_type=jnp.float32)
    lat_grad = (
        jnp.einsum("td,fd->tf", err_grad, dec_w, preferred_element_type=jnp.float32)
        + l1_coeff * token_weight[:, None]
    )
    pre_grad = jnp.where(pre_acts > 0.0, lat_grad, jnp.zeros_like(lat_grad)).astype(jnp.bfloat16)
    enc_grad = jnp.einsum("td,tf->df", scaled, pre_grad, preferred_element_type=jnp.float32)
    local_total = jnp.sum(enc_grad * enc_grad) + jnp.sum(dec_grad * dec_grad)
    grad_total = lax.psum(local_total, ("src", "feat"))
    clip_factor = lax.rsqrt(grad_total + 1e-12)
    enc_update = adam_direction(enc_grad, enc_first, enc_second, clip_factor)
    dec_update = adam_direction(dec_grad, dec_first, dec_second, clip_factor)
    return (enc_update, dec_update)


def solution(mesh):
    in_specs = (
        P(None, "src"),
        P(),
        P("src"),
        P("src", "feat"),
        P("src", "feat"),
        P("feat", "src"),
        P(None, ("src", "feat")),
        P(("src", "feat")),
        P(("src", "feat"), None),
        P(),
        P(None, ("src", "feat")),
        P(None, ("src", "feat")),
        P(("src", "feat"), None),
        P(("src", "feat"), None),
    )
    out_specs = (P(None, ("src", "feat")), P(("src", "feat"), None))
    return jax.shard_map(local, mesh=mesh, in_specs=in_specs, out_specs=out_specs, check_vma=False)
```

profile of v0, /device:TPU:1, one launch (start us, length us, event | category | flops | bytes accessed | tf_op | source)
XLA Modules:
  0.0 1579.8 jit_solution(12227848700793156754)
XLA Ops:
  7.2 1.1 fusion.17
  8.4 16.8 %psum.42 = f32[448]{0:T(512)S(1)} all-reduce(f32[448]{0:T(512)S(1)} %fusion.17), channel_id=1, replica_groups=mesh['src'=8,'feat'=64] {'src'}, use_global_device_ids=true, to_apply=%region_1.0 | all-reduce | flops 448 | bytes 3584 | tf_op jit(solution)/shard_map/psum | solution.py:47
  25.2 0.7 convert_element_type.68
  25.9 2.2 fusion.39
  28.1 1.2 fusion.41
  29.4 96.6 %all-reduce.10.cloned.1.call-done = (f32[448,288]{0,1:T(8,128)}, f32[448,288]{0,1:T(8,128)}) async-done(((f32[448,288]{0,1:T(8,128)}, f32[448,288]{0,1:T(8,128)}), (f32[448,288]{0,1:T(8,128)}, f32[448,288]{0,1:T(8,128)})) %all-reduce.10.cloned.1.call-update) | async-done | bytes 1032208 | tf_op jit(solution)/shard_map/psum | solution.py:52
  126.0 2.5 fusion.30
  128.6 0.0 all-gather.5.cloned.1.call-start
  128.6 487.3 %all-reduce.6.cloned.1.call-done = f32[448,288]{0,1:T(8,128)} async-done(((f32[448,288]{0,1:T(8,128)}), f32[448,288]{0,1:T(8,128)}) %all-reduce.6.cloned.1.call-update) | async-done | bytes 516112 | tf_op jit(solution)/shard_map/psum | solution.py:55
  616.0 1.2 fusion.15
  617.2 14.9 psum.46
  632.1 0.8 fusion.16
  633.0 56.7 %all-gather.5.cloned.1.call-done = bf16[448,2304]{0,1:T(8,128)(2,1)} async-done(((bf16[448,288]{0,1:T(8,128)(2,1)}), bf16[448,2304]{0,1:T(8,128)(2,1)}) %all-gather.5.cloned.1.call-update) | async-done | bytes 2064400 | tf_op jit(solution)/shard_map/all_gather | solution.py:62
  689.7 2.5 convolution_add_fusion.1
  692.2 3.0 fusion.45
  695.2 1.3 dynamic-slice
  697.2 534.5 %all-reduce.8.cloned.1.call-done = f32[448,2304]{0,1:T(8,128)} async-done(((f32[448,2304]{0,1:T(8,128)}), f32[448,2304]{0,1:T(8,128)}) %all-reduce.8.cloned.1.call-update) | async-done | bytes 4128784
  1231.7 3.2 constant_dynamic-slice_fusion
  1235.0 0.8 dynamic-slice.2
  1235.8 35.5 %reduce-scatter.3.cloned.1.call-done = f32[7,288]{0,1:T(8,128)} async-done(((f32[7,2304]{0,1:T(8,128)}), f32[7,288]{0,1:T(8,128)}) %reduce-scatter.3.cloned.1.call-update) | async-done | bytes 8080 | tf_op jit(solution)/shard_map/reduce_scatter | solution.py:70
  1271.3 1.0 fusion.43
  1272.3 0.1 copy.22
  1272.4 22.1 %all-gather = bf16[8,288,7]{1,2,0:T(8,128)(2,1)S(1)} all-gather(bf16[1,288,7]{1,2,0:T(8,128)(2,1)S(1)} %copy.22), channel_id=1, replica_groups=mesh['src'=8,'feat'=64] {'src'}, dimensions={0}, use_global_device_ids=true | all-gather | bytes 36288 | tf_op jit(solution)/shard_map/all_gather | solution.py:75
  1294.6 0.7 reshape.14
  1295.3 0.6 convert_reduce_fusion
  1296.6 154.3 %all-gather.7.cloned.1.call-done = bf16[64,7,2304]{2,1,0:T(8,128)(2,1)} async-done(((bf16[1,7,2304]{2,1,0:T(8,128)(2,1)}), bf16[64,7,2304]{2,1,0:T(8,128)(2,1)}) %all-gather.7.cloned.1.call-update) | async-done | bytes 2064400 | tf_op jit(solution)/shard_map/all_gather | solution.py:76
  1450.9 4.4 reshape.17
  1455.3 4.4 multiply_reduce_fusion
  1459.7 5.3 multiply_reduce_fusion.1
  1466.4 100.7 %psum.47 = f32[]{:T(128)} all-reduce(f32[]{:T(128)S(6)} %add.98), channel_id=1, replica_groups=mesh['src'=8,'feat'=64] {'src','feat'}, use_global_device_ids=true, to_apply=%region_12.13 | all-reduce | flops 1 | bytes 8 | tf_op jit(solution)/shard_map/psum | solution.py:88
  1567.8 3.4 fusion.10
  1571.3 1.7 fusion.11
  (40 shorter events, 0.4 us)
Async XLA Ops:
  7.2 685.0 %copy-start = (bf16[128,2304]{1,0:T(8,128)(2,1)S(1)}, bf16[128,2304]{1,0:T(8,128)(2,1)}, u32[]{:S(2)}) copy-start(bf16[128,2304]{1,0:T(8,128)(2,1)} %param.22) | copy-start | bytes 1769476
  7.2 20.9 %copy-start.2 = (bf16[448,288]{0,1:T(8,128)(2,1)S(1)}, bf16[448,288]{0,1:T(8,128)(2,1)}, u32[]{:S(2)}) copy-start(bf16[448,288]{0,1:T(8,128)(2,1)} %param.14) | copy-start | bytes 774148
  7.2 20.9 %copy-start.8 = (bf16[288,288]{1,0:T(8,128)(2,1)S(1)}, bf16[288,288]{1,0:T(8,128)(2,1)}, u32[]{:S(2)}) copy-start(bf16[288,288]{1,0:T(8,128)(2,1)} %param.17) | copy-start | bytes 497668
  7.2 118.8 %all-reduce.10.cloned.1.call-start = ((), (), s32[]{:S(2)}) async-start(), calls=%async_computation.6 | async-start | bytes 2359296 | tf_op jit(solution)/shard_map/psum | solution.py:52
  28.1 97.9 %copy-start.9 = (bf16[288,288]{1,0:T(8,128)(2,1)S(1)}, bf16[288,288]{1,0:T(8,128)(2,1)}, u32[]{:S(2)}) copy-start(bf16[288,288]{1,0:T(8,128)(2,1)} %param.19) | copy-start | bytes 497668
  29.4 586.6 %all-reduce.6.cloned.1.call-start = ((), (), s32[]{:S(2)}) async-start(), calls=%async_computation.1 | async-start | bytes 1179648 | tf_op jit(solution)/shard_map/psum | solution.py:55
  128.6 561.1 %copy-start.5 = (bf16[2304,128]{1,0:T(8,128)(2,1)S(1)}, bf16[2304,128]{1,0:T(8,128)(2,1)}, u32[]{:S(2)}) copy-start(bf16[2304,128]{1,0:T(8,128)(2,1)} %param.20) | copy-start | bytes 1769476
  128.6 504.4 %copy-start.11 = (bf16[128]{0:T(256)(128)(2,1)S(1)}, bf16[128]{0:T(256)(128)(2,1)}, u32[]{:S(2)}) copy-start(bf16[128]{0:T(256)(128)(2,1)} %param.21) | copy-start | bytes 772
  128.6 561.1 %all-gather.5.cloned.1.call-start = ((), (), s32[]{:S(2)}) async-start(), calls=%async_computation.2 | async-start | bytes 2654208 | tf_op jit(solution)/shard_map/all_gather | solution.py:62
  616.0 16.1 %copy-start.4 = (f32[448,288]{0,1:T(8,128)S(1)}, f32[448,288]{0,1:T(8,128)}, u32[]{:S(2)}) copy-start(f32[448,288]{0,1:T(8,128)} %all-reduce.6.cloned.1.call-done) | copy-start | bytes 1548292
  632.9 598.8 %all-reduce.8.cloned.1.call-start = ((), (), s32[]{:S(2)}) async-start(), calls=%async_computation.5 | async-start | bytes 9437184
  695.2 576.1 %reduce-scatter.3.cloned.1.call-start = ((), (), s32[]{:S(2)}) async-start(), calls=%async_computation.3 | async-start | bytes 1327104 | tf_op jit(solution)/shard_map/reduce_scatter | solution.py:70
  1231.7 39.6 %copy-start.1 = (bf16[448,2304]{0,1:T(8,128)(2,1)S(1)}, bf16[448,2304]{0,1:T(8,128)(2,1)}, u32[]{:S(2)}) copy-start(bf16[448,2304]{0,1:T(8,128)(2,1)} %all-gather.5.cloned.1.call-done) | copy-start | bytes 6193156
  1234.9 60.4 %copy-start.10 = (s32[448]{0:T(512)S(1)}, s32[448]{0:T(512)}, u32[]{:S(2)}) copy-start(s32[448]{0:T(512)} %param.15) | copy-start | bytes 5380
  1235.0 215.9 %all-gather.7.cloned.1.call-start = ((), (), s32[]{:S(2)}) async-start(), calls=%async_computation.4 | async-start | bytes 2396160 | tf_op jit(solution)/shard_map/all_gather | solution.py:76
  1567.8 3.5 copy-start.3
  1567.8 3.5 copy-start.6
  1567.8 3.4 copy-start.7
Sparse Core Ops, SparseCore 0:
  29.5 96.4 all-reduce.9
  129.5 486.4 all-reduce.5
  633.1 56.5 all-gather.4
  695.3 536.3 all-reduce.7
  1235.1 36.1 reduce-scatter.2
  1295.4 155.4 all-gather.6
where the time goes:
time: 1580 us
  waiting for transfers between devices  1360 us (86%)
  blocking collectives  155 us (10%)
  matrix products  21.2 us (1%)
  between operations  17.6 us (1%)
    unnamed x7, waiting for transfers between devices  535 us
    psum x1, waiting for transfers between devices, local(): ffn_out = lax.psum(out_part, 'feat')  487 us
    all_gather x1, waiting for transfers between devices, local(): errors = lax.all_gather(err_cols, 'feat', axis=0, tiled=True)  154 us
    psum x1, blocking collectives, local(): grad_total = lax.psum(local_total, ('src', 'feat'))  101 us
    psum x1, waiting for transfers between devices, local(): gate_acts, up_acts = lax.psum((gate_part, up_part), 'src')  96.6 us
    all_gather x1, waiting for transfers between devices, local(): scaled = lax.all_gather(scaled_part, 'src', axis=1, tiled=True)  56.7 us
    reduce_scatter x1, waiting for transfers between devices, local(): lax.psum_scatter(row_share, 'src', scatter_dimension=1, tiled=True)  35.5 us
  transfers between devices with their start and end apart: 6, of which 6 were waited for; matrix products, arithmetic and copies ran while one was open for 0% of the time, Pallas kernels for 0%

commit v1 on v0

v1 whole, which is shorter than its diff:
```python
import functools

import jax
import jax.numpy as jnp
from jax import lax
from jax.experimental import pallas as pl
from jax.experimental.pallas import tpu as pltpu
from jax.sharding import PartitionSpec as P

SPECIAL = 4
TOK = 448
HALF = 224
D = 2304
W = 288
ZN = 16
SRC = 8
FEAT = 64

eps_rms = 1e-06
beta_one = 0.9
beta_two = 0.999
adam_count = 100.0
l1_coeff = 0.2

F32 = jnp.float32
BF16 = jnp.bfloat16


def tiles(v):
    return v.reshape(v.shape[0] // 16, 16, 128)


def rows(v):
    return v.reshape(v.shape[0] * 16, 128)


def dot(a, b, ca=1, cb=0):
    return lax.dot_general(a, b, (((ca,), (cb,)), ((), ())), preferred_element_type=F32)


def lane_group(shape):
    return lax.broadcasted_iota(jnp.int32, shape, len(shape) - 1)


def fold(read, lanes):
    out = read(3)
    for g in (2, 1, 0):
        out = jnp.where(lanes < 32 * (g + 1), read(g), out)
    return out


def adam(grad, first, second, clip):
    scaled_grad = clip * grad
    first_new = beta_one * first.astype(F32) + (1.0 - beta_one) * scaled_grad
    second_new = beta_two * second.astype(F32) + (1.0 - beta_two) * scaled_grad * scaled_grad
    corr_one = 1.0 - beta_one**adam_count
    corr_two = 1.0 - beta_two**adam_count
    return (first_new / corr_one / (jnp.sqrt(second_new / corr_two) + 1e-08)).astype(BF16)


def kernel(
    res, tok, gain, gw, uw, dw_h, ew_h, eb, dcw_h, db, ef_h, es_h, df_h, ds_h,
    eo, do,
    dw, ew, dcw, ef, es, df, ds, ebx,
    rn, rt, gu, p1r, sqs, sqr, hb, hh, dwf, tail, rest, ot, p3r,
    gs, ss, twb, bias, pa, lat_t, tt, p5r, aa, p5z, ee, st,
    dg, dgs, dgr, eg, egs, egr, n7, n7z, n7x, n7c,
    lsem, wsend, wrecv, ssem, rsem,
):
    s = lax.axis_index("src")
    f = lax.axis_index("feat")
    c = lax.rem(f, 2)
    q = lax.div(f, 2)
    z = lax.rem(q, ZN)
    yhi = lax.div(q, ZN)
    xy = s * 2 + yhi
    half = lax.div(s, 4)

    def to(src, feat):
        return {"device_id": (src, feat), "device_id_type": pl.DeviceIdType.MESH}

    other = to(s, q * 2 + 1 - c)

    def src_peer(d, core):
        return to(lax.rem(s + d, SRC), q * 2 + core)

    def q_peer(d):
        return to(s, lax.rem(q + d, 32) * 2 + c)

    def z_peer(d):
        return to(s, (yhi * ZN + lax.rem(z + d, ZN)) * 2 + c)

    def xy_peer(d):
        i = lax.rem(xy + d, 16)
        return to(lax.div(i, 2), (lax.rem(i, 2) * ZN + z) * 2 + c)

    def loop(n, fn):
        def body(d, carry):
            fn(d)
            return carry

        lax.fori_loop(1, n, body, 0)

    def send(src, dst, k, where):
        pltpu.make_async_remote_copy(
            src_ref=src, dst_ref=dst, send_sem=ssem.at[k], recv_sem=rsem.at[k], **where
        ).start()

    def arrived(ref, k):
        pltpu.make_async_copy(ref, ref, rsem.at[k]).wait()

    def left(ref, k):
        pltpu.make_async_copy(ref, ref, ssem.at[k]).wait()

    barrier = pltpu.get_barrier_semaphore()
    pl.semaphore_signal(barrier, inc=1, **other)

    def greet(d):
        pl.semaphore_signal(barrier, inc=1, **src_peer(d, c))
        pl.semaphore_signal(barrier, inc=1, **src_peer(d, 1 - c))
        pl.semaphore_signal(
            barrier, inc=1, **to(lax.rem(s + d, SRC), (lax.rem(yhi + 1, 2) * ZN + z) * 2 + c)
        )

    loop(SRC, greet)
    loop(32, lambda d: pl.semaphore_signal(barrier, inc=1, **q_peer(d)))

    loads = []
    for k, (src, dst) in enumerate(
        ((dw_h, dw), (ew_h, ew.at[0]), (dcw_h, dcw.at[0]), (ef_h, ef), (es_h, es), (df_h, df), (ds_h, ds))
    ):
        cp = pltpu.make_async_copy(src, dst, lsem.at[k])
        cp.start()
        loads.append(cp)

    lanes = lane_group((64, 128))
    wide = lane_group((128, 128))
    pick = jnp.where(
        jnp.bitwise_and(lane_group((32, 128)), 31) == lax.broadcasted_iota(jnp.int32, (32, 128), 0), 1.0, 0.0
    ).astype(BF16)

    resf = res[...].astype(F32)
    xg = (resf * gain[...].astype(F32)).astype(BF16)
    for k, w in enumerate((gw, uw)):
        main = dot(xg, w[:, 0:256])
        spread = dot(w[:, 256:288], pick).astype(BF16)
        tail[0:448] = dot(xg, spread)
        tail[448:512] = jnp.zeros((64, 128), F32)
        for h in range(2):
            for j in range(2):
                gu[k, h * 32 + 14 * j : h * 32 + 14 * j + 14] = tiles(
                    main[224 * h : 224 * h + 224, 128 * j : 128 * j + 128].astype(BF16)
                )
            part = fold(lambda g: tail[224 * h + 64 * g : 224 * h + 64 * g + 64], lanes)
            gu[k, h * 32 + 28 : h * 32 + 32] = tiles(part.astype(BF16))
    squares = jnp.sum(resf * resf, axis=1, keepdims=True)
    squares = jnp.concatenate([squares, jnp.zeros((64, 1), F32)], axis=0)
    cols = jnp.zeros((128, 128), F32)
    for k in range(4):
        cols = jnp.where(wide == k, squares[128 * k : 128 * k + 128], cols)
    sqs[...] = cols.T[0:8]

    pl.semaphore_wait(barrier, 53)

    def send_p1(d):
        t = lax.rem(s + d, SRC)
        send(gu.at[:, pl.ds(8 * t, 8)], p1r.at[d - 1], 0, src_peer(d, c))
        send(sqs, sqr.at[d - 1], 1, src_peer(d, c))

    loop(SRC, send_p1)

    ids = tok[...]
    live = jnp.where(ids >= SPECIAL, 1.0, 0.0)
    weight = live / jnp.maximum(jnp.sum(live), 1.0)
    weight = jnp.concatenate([weight, jnp.zeros((1, 64), F32)], axis=1)
    weight = jnp.concatenate(
        [weight[:, 128 * k : 128 * k + 128] for k in range(4)] + [jnp.zeros((124, 128), F32)], axis=0
    ).T
    for k in range(4):
        twb[128 * k : 128 * k + 128] = jnp.broadcast_to(weight[:, k : k + 1], (128, 128))
    for k in range(18):
        bias[k] = jnp.broadcast_to(db[:, 128 * k : 128 * k + 128].astype(F32), (8, 128))
    ebx[0] = jnp.broadcast_to(eb[...].astype(F32), (8, 128))

    def share(ref, k):
        return pltpu.make_async_remote_copy(
            src_ref=ref.at[0], dst_ref=ref.at[1], send_sem=wsend.at[k], recv_sem=wrecv.at[k], **other
        )

    shares = [share(ebx, 0), share(dwf, 1), share(ew, 2), share(dcw, 3)]
    shares[0].start()
    loads[0].wait()
    spread = dot(dw[:, 256:288], pick).astype(BF16)
    dwf[0, 0:256, 0:256] = dw[0:256, 0:256]
    dwf[0, 0:256, 256:384] = spread[0:256]
    for g in range(4):
        dwf[0, 256 + 32 * g : 288 + 32 * g, 0:256] = dw[256:288, 0:256]
        dwf[0, 256 + 32 * g : 288 + 32 * g, 256:384] = spread[256:288]
    shares[1].start()
    loads[1].wait()
    shares[2].start()
    loads[2].wait()
    shares[3].start()

    off = pl.multiple_of(HALF * c, 32)
    for j in range(2):
        rest[14 * j : 14 * j + 14] = tiles(res[pl.ds(off, HALF), 128 * j : 128 * j + 128].astype(F32))
    tail[0:448] = dot(res[:, 256:288], pick)
    tail[448:512] = jnp.zeros((64, 128), F32)
    rest[28:32] = tiles(fold(lambda g: tail[pl.ds(off + 64 * g, 64)], lanes))
    ss[252:256] = jnp.zeros((4, 16, 128), BF16)
    tt[252:256] = jnp.zeros((4, 16, 128), BF16)

    arrived(sqr, 1)
    total = sqs[...]
    for d in range(7):
        total = total + sqr[d]
    inv = lax.rsqrt(total / D + eps_rms)
    inv = jnp.concatenate([inv, jnp.zeros((120, 128), F32)], axis=0).T
    for k in range(4):
        rn[128 * k : 128 * k + 128] = jnp.broadcast_to(inv[:, k : k + 1], (128, 128))
    for h in range(2):
        for j in range(2):
            rt[h * 32 + 14 * j : h * 32 + 14 * j + 14] = tiles(rn[224 * h : 224 * h + 224])
        rt[h * 32 + 28 : h * 32 + 32] = tiles(
            fold(lambda g: rn[224 * h + 64 * g : 224 * h + 64 * g + 64], lanes)
        )

    arrived(p1r, 0)
    acts = []
    for k in range(2):
        acc = gu[k, pl.ds(8 * s, 8)].astype(F32)
        for d in range(7):
            acc = acc + p1r[d, k].astype(F32)
        acts.append(acc * rt[pl.ds(8 * s, 8)])
    hb[...] = (jax.nn.gelu(acts[0], approximate=True) * acts[1]).astype(BF16)

    slot = jnp.where(c == half, 0, 1)
    place = hh.at[slot, pl.ds(8 * lax.rem(s, 4), 8)]

    @pl.when(c == half)
    def _():
        pltpu.make_async_copy(hb, place, rsem.at[2]).start()

    @pl.when(c != half)
    def _():
        send(hb, place, 2, src_peer(0, half))

    loop(SRC, lambda d: send(hb, place, 2, src_peer(d, half)))
    shares[1].wait()
    arrived(hh, 2)
    acc = jnp.zeros((HALF, 384), F32)
    for k in range(2):
        last = rows(hh[k, 28:32])
        keep = jnp.zeros_like(last)
        split = jnp.concatenate(
            [jnp.where((lanes >= 32 * g) & (lanes < 32 * g + 32), last, keep) for g in range(4)], axis=0
        )[0:HALF]
        lhs = jnp.concatenate([rows(hh[k, 0:14]), rows(hh[k, 14:28]), split], axis=1)
        acc = acc + dot(lhs, dwf[k])
    for j in range(2):
        ot[14 * j : 14 * j + 14] = tiles(acc[:, 128 * j : 128 * j + 128].astype(BF16))
    tail[0:224] = acc[:, 256:384]
    tail[224:256] = jnp.zeros((32, 128), F32)
    ot[28:32] = tiles(fold(lambda g: tail[64 * g : 64 * g + 64], lanes).astype(BF16))

    loop(32, lambda d: send(ot.at[lax.rem(q + d, 32)], p3r.at[d - 1], 3, q_peer(d)))
    arrived(p3r, 3)
    acc = ot[q].astype(F32)
    for d in range(31):
        acc = acc + p3r[d].astype(F32)
    gs[xy * 16 + z] = (rest[q] + acc).astype(BF16)

    mine = gs.at[xy * 16 + z]
    loop(ZN, lambda d: send(mine, mine, 4, z_peer(d)))
    arrived(gs.at[0:15], 4)
    block = gs.at[pl.ds(xy * 16, 16)]
    loop(16, lambda d: send(block, block, 5, xy_peer(d)))
    arrived(gs.at[0:240], 5)

    acc = jnp.zeros((HALF, 128), F32)
    rem = jnp.zeros((64, 128), F32)
    for k in range(SRC):
        for j in range(2):
            v = rows(gs[32 * k + 14 * j : 32 * k + 14 * j + 14]).astype(F32)
            acc = acc + v * v
        v = rows(gs[32 * k + 28 : 32 * k + 32]).astype(F32)
        rem = rem + v * v
    acc = acc + jnp.concatenate(
        [jnp.where((lanes >= 32 * g) & (lanes < 32 * g + 32), rem, 0.0) for g in range(4)], axis=0
    )[0:HALF]
    inv = lax.rsqrt(jnp.sum(acc, axis=1, keepdims=True) / D + eps_rms)
    tall = lane_group((HALF, 128))

    def turn(v, by):
        by = by % 128
        return v if by == 0 else pltpu.roll(v, by, 1)

    for k in range(SRC):
        m, base = k % 4, 9 * (k // 4)
        a0 = turn(rows(gs[32 * k : 32 * k + 14]).astype(F32) * inv, 32 * m)
        a1 = turn(rows(gs[32 * k + 14 : 32 * k + 28]).astype(F32) * inv, 32 * m)
        last = rows(gs[32 * k + 28 : 32 * k + 32]).astype(F32)
        rem = jnp.concatenate([turn(last, 32 * m - 32 * g) for g in range(4)], axis=0)[0:HALF] * inv
        if m == 0:
            first, second = a0, a1
        else:
            first = jnp.where(tall < 32 * m, carry, a0)
            second = jnp.where(tall < 32 * m, a0, a1)
        carry = jnp.where(tall < 32 * m, a1, rem)
        for at, v in ((2 * m, first), (2 * m + 1, second)) + (((8, carry),) if m == 3 else ()):
            ss[14 * (base + at) : 14 * (base + at) + 14] = tiles(v.astype(BF16))

    def cols_of(ref, p):
        return jnp.concatenate([rows(ref[28 * p : 28 * p + 14]), rows(ref[28 * p + 14 : 28 * p + 28])], axis=1)

    for k in (0, 2, 3):
        shares[k].wait()
    acc = jnp.zeros((HALF, 256), F32)
    for p in range(9):
        rhs = jnp.concatenate([ew[0, 256 * p : 256 * p + 256], ew[1, 256 * p : 256 * p + 256]], axis=1)
        acc = acc + dot(cols_of(ss, p), rhs)
    acc = acc + jnp.concatenate([ebx[0, 0:1], ebx[1, 0:1]], axis=1)
    pa[...] = acc
    latents = jnp.maximum(acc, 0.0)
    lat = latents.astype(BF16)
    for p in range(9):
        rhs = jnp.concatenate([dcw[0, :, 256 * p : 256 * p + 256], dcw[1, :, 256 * p : 256 * p + 256]], axis=0)
        r = dot(lat, rhs).astype(BF16)
        tt[28 * p : 28 * p + 14] = tiles(r[:, 0:128])
        tt[28 * p + 14 : 28 * p + 28] = tiles(r[:, 128:256])

    loop(16, lambda d: send(tt.at[pl.ds(16 * lax.rem(xy + d, 16), 16)], p5r.at[d - 1], 6, xy_peer(d)))
    lat_t[...] = jnp.concatenate([latents, jnp.zeros((32, 256), F32)], axis=0).T.astype(BF16)
    for p in range(18):
        v = rows(ss[14 * p : 14 * p + 14]).astype(F32)
        st[128 * p : 128 * p + 128] = jnp.concatenate([v, jnp.zeros((32, 128), F32)], axis=0).T.astype(BF16)
    arrived(p5r, 6)

    def add_up(k, carry):
        acc = tt[16 * xy + k].astype(F32)
        for d in range(15):
            acc = acc + p5r[d, k].astype(F32)
        aa[k] = acc.astype(BF16)
        return carry

    lax.fori_loop(0, 16, add_up, 0)
    loop(ZN, lambda d: send(aa.at[lax.rem(z + d, ZN)], p5z.at[d - 1], 7, z_peer(d)))
    arrived(p5z, 7)
    acc = aa[z].astype(F32)
    for d in range(15):
        acc = acc + p5z[d].astype(F32)
    t = xy * 16 + z
    col = jnp.minimum(lax.div(t, 14), 17)
    row = lax.rem(t, 14)
    err = (acc + bias[col, 0:1] - ss[t].astype(F32)).astype(BF16)
    tw = twb[pl.ds(pl.multiple_of(off + 16 * row, 16), 16)]
    ee[t] = (2.0 * tw * err.astype(F32)).astype(BF16)
    mine2 = ee.at[t]
    loop(ZN, lambda d: send(mine2, mine2, 8, z_peer(d)))
    arrived(ee.at[0:15], 8)
    block2 = ee.at[pl.ds(xy * 16, 16)]
    loop(16, lambda d: send(block2, block2, 9, xy_peer(d)))
    arrived(ee.at[0:240], 9)

    lt = lat_t[:, 0:HALF]
    acc = jnp.zeros((HALF, 256), F32)
    for p in range(9):
        r = dot(lt, cols_of(ee, p))
        dg[:, 256 * p : 256 * p + 256] = r[0:128]
        dgs[:, 256 * p : 256 * p + 256] = r[128:256].astype(BF16)
    send(dgs, dgr, 10, other)
    for p in range(9):
        rhs = jnp.concatenate([dcw[0, :, 256 * p : 256 * p + 256], dcw[1, :, 256 * p : 256 * p + 256]], axis=0)
        acc = acc + dot(cols_of(ee, p), rhs, 1, 1)
    tw = l1_coeff * twb[pl.ds(off, HALF)]
    acc = acc + jnp.concatenate([tw, tw], axis=1)
    pg = jnp.where(pa[...] > 0.0, acc, 0.0).astype(BF16)
    for p in range(9):
        r = dot(st[256 * p : 256 * p + 256, 0:HALF], pg)
        eg[256 * p : 256 * p + 256] = r[:, 0:128]
        egs[256 * p : 256 * p + 256] = r[:, 128:256].astype(BF16)
    send(egs, egr, 11, other)
    arrived(dgr, 10)
    acc = jnp.zeros((8, 128), F32)
    for p in range(18):
        v = dg[:, 128 * p : 128 * p + 128] + dgr[:, 128 * p : 128 * p + 128].astype(F32)
        dg[:, 128 * p : 128 * p + 128] = v
        acc = acc + jnp.sum((v * v).reshape(16, 8, 128), axis=0)
    arrived(egr, 11)
    for p in range(18):
        v = eg[128 * p : 128 * p + 128] + egr[128 * p : 128 * p + 128].astype(F32)
        eg[128 * p : 128 * p + 128] = v
        acc = acc + jnp.sum((v * v).reshape(16, 8, 128), axis=0)

    n7[0] = acc
    loop(ZN, lambda d: send(n7.at[0], n7z.at[d - 1], 12, z_peer(d)))
    for k in range(3, 7):
        loads[k].wait()
    arrived(n7z, 12)
    for d in range(15):
        acc = acc + n7z[d]
    n7[1] = acc
    loop(16, lambda d: send(n7.at[1], n7x.at[d - 1], 13, xy_peer(d)))
    arrived(n7x, 13)
    for d in range(15):
        acc = acc + n7x[d]
    n7[2] = acc
    send(n7.at[2], n7c, 14, other)
    arrived(n7c, 14)
    acc = acc + n7c[...]
    clip = lax.rsqrt(jnp.sum(acc, keepdims=True) + 1e-12)

    for p in range(18):
        at = slice(128 * p, 128 * p + 128)
        do[:, at] = adam(dg[:, at], df[:, at], ds[:, at], clip)
        eo[at] = adam(eg[at], ef[at], es[at], clip)

    left(p1r, 0)
    left(sqr, 1)

    @pl.when(c == half)
    def _():
        left(hh.at[0, 0:28], 2)
        left(hh.at[1, 0:28], 2)

    @pl.when(c != half)
    def _():
        left(hh, 2)

    left(p3r, 3)
    left(gs.at[0:15], 4)
    left(gs.at[0:240], 5)
    left(p5r, 6)
    left(p5z, 7)
    left(ee.at[0:15], 8)
    left(ee.at[0:240], 9)
    left(dgs, 10)
    left(egs, 11)
    left(n7z, 12)
    left(n7x, 13)
    left(n7c, 14)


def local(
    residual, token_ids, ffn_gain, gate_w, up_w, down_w, enc_w, enc_bias, dec_w, dec_bias,
    enc_first, enc_second, dec_first, dec_second,
):
    vm = pl.BlockSpec(memory_space=pltpu.VMEM)
    hbm = pl.BlockSpec(memory_space=pl.ANY)
    V = pltpu.VMEM
    scratch = [
        V((W, W), BF16), V((2, D, 128), BF16), V((2, 128, D), BF16),
        V((D, 128), BF16), V((D, 128), BF16), V((128, D), BF16), V((128, D), BF16), V((2, 8, 128), F32),
        V((512, 128), F32), V((64, 16, 128), F32), V((2, 64, 16, 128), BF16), V((7, 2, 8, 16, 128), BF16),
        V((8, 128), F32), V((7, 8, 128), F32), V((8, 16, 128), BF16), V((2, 32, 16, 128), BF16),
        V((2, 384, 384), BF16), V((512, 128), F32), V((32, 16, 128), F32), V((32, 16, 128), BF16),
        V((31, 16, 128), BF16),
        V((256, 16, 128), BF16), V((256, 16, 128), BF16), V((512, 128), F32), V((18, 8, 128), F32),
        V((HALF, 256), F32), V((256, 256), BF16), V((256, 16, 128), BF16), V((15, 16, 16, 128), BF16),
        V((16, 16, 128), BF16), V((15, 16, 128), BF16), V((256, 16, 128), BF16), V((D, 256), BF16),
        V((128, D), F32), V((128, D), BF16), V((128, D), BF16),
        V((D, 128), F32), V((D, 128), BF16), V((D, 128), BF16),
        V((3, 8, 128), F32), V((15, 8, 128), F32), V((15, 8, 128), F32), V((8, 128), F32),
        pltpu.SemaphoreType.DMA((7,)), pltpu.SemaphoreType.DMA((4,)), pltpu.SemaphoreType.DMA((4,)),
        pltpu.SemaphoreType.DMA((15,)), pltpu.SemaphoreType.DMA((15,)),
    ]
    return pl.pallas_call(
        kernel,
        out_shape=(jax.ShapeDtypeStruct((D, 128), BF16), jax.ShapeDtypeStruct((128, D), BF16)),
        in_specs=[vm, vm, vm, vm, vm, hbm, hbm, vm, hbm, vm, hbm, hbm, hbm, hbm],
        out_specs=(vm, vm),
        scratch_shapes=scratch,
        compiler_params=pltpu.CompilerParams(
            collective_id=0, has_side_effects=True, vmem_limit_bytes=48 << 20
        ),
    )(
        residual, token_ids.reshape(1, TOK), ffn_gain.reshape(1, W), gate_w, up_w, down_w, enc_w,
        enc_bias.reshape(1, 128), dec_w, dec_bias.reshape(1, D), enc_first, enc_second, dec_first, dec_second,
    )


def solution(mesh):
    in_specs = (
        P(None, "src"),
        P(),
        P("src"),
        P("src", "feat"),
        P("src", "feat"),
        P("feat", "src"),
        P(None, ("src", "feat")),
        P(("src", "feat")),
        P(("src", "feat"), None),
        P(),
        P(None, ("src", "feat")),
        P(None, ("src", "feat")),
        P(("src", "feat"), None),
        P(("src", "feat"), None),
    )
    out_specs = (P(None, ("src", "feat")), P(("src", "feat"), None))
    return jax.shard_map(local, mesh=mesh, in_specs=in_specs, out_specs=out_specs, check_vma=False)
```

time: 1580 us -> 144 us (0.09)
  waiting for transfers between devices: 1360 us -> 0 us
  blocking collectives: 155 us -> 0 us
  Pallas kernels: 0 us -> 131 us
  matrix products: 21.2 us -> 0 us
  between operations: 17.6 us -> 0.72 us
    psum x2 -> x0, waiting for transfers between devices: 584 us -> none  [the longest x1 487 us: local(): ffn_out = lax.psum(out_part, 'feat')]
    unnamed x7 -> x0, waiting for transfers between devices: 535 us -> none
    all_gather x2 -> x0, waiting for transfers between devices: 211 us -> none  [the longest x1 154 us: local(): errors = lax.all_gather(err_cols, 'feat', axis=0, tiled=True)]
    psum x3 -> x0, blocking collectives: 132 us -> none  [the longest x1 101 us: local(): grad_total = lax.psum(local_total, ('src', 'feat'))]
    pallas_call x0 -> x1, Pallas kernels: none -> 131 us  [local(): pl.pallas_call(kernel, out_shape=(jax.ShapeDtypeStruct((D, 128), BF16), j...]
    reduce_scatter x1 -> x0, waiting for transfers between devices: 35.5 us -> none  [local(): lax.psum_scatter(row_share, 'src', scatter_dimension=1, tiled=True)]
    all_gather x1 -> x0, blocking collectives: 22.1 us -> none  [local(): err_cols = lax.all_gather(err_block, 'src', axis=1, tiled=True)]
    dot_general x7 -> x0, matrix products: 21.2 us -> none  [the longest x1 5.35 us: local(): jnp.einsum('td,tf->df', scaled, pre_grad, preferred_element_type=jnp.floa...]
  transfers between devices with their start and end apart: 6 -> 0, of which waited for: 6 -> 0; matrix products, arithmetic and copies ran while one was open for 0% -> 0% of each run, Pallas kernels for 0% -> 0%
where the time goes in v1:
time: 144 us
  Pallas kernels  131 us (91%)
  local copies, waits for them, and re-layouts  11.7 us (8%)
    pallas_call x1, Pallas kernels, local(): pl.pallas_call(kernel, out_shape=(jax.ShapeDtypeStruct((D, 128), BF16), j...  131 us
    unnamed x27, local copies, waits for them, and re-layouts  11 us

profile of v1, /device:TPU:1, one launch (start us, length us, event | category | flops | bytes accessed | tf_op | source)
XLA Modules:
  0.0 143.8 jit_solution(14726398248511826886)
XLA Ops:
  0.6 0.0 copy-start.11
  0.6 0.0 copy-start
  0.7 0.7 reshape.17.gain
  1.4 0.0 copy-done.11
  1.4 0.0 copy-start.9
  1.4 0.0 copy-start.10
  1.4 1.2 copy.16.res
  2.6 0.0 copy-done
  2.7 0.0 copy-done.9
  2.7 0.0 copy-done.10
  2.7 0.0 copy-start.1
  2.7 1.1 copy-done.1
  3.7 0.0 copy-start.2
  3.7 1.1 copy-done.2
  4.8 0.0 copy-start.3
  4.8 1.1 copy-done.3
  5.9 0.0 copy-start.4
  5.9 1.1 copy-done.4
  6.9 0.0 copy-start.5
  6.9 1.1 copy-done.5
  8.0 0.0 copy-start.6
  8.0 0.9 copy-done.6
  8.9 0.0 copy-start.7
  8.9 0.9 copy-done.7
  9.9 0.0 copy-start.8
  9.9 0.9 copy-done.8
  10.8 131.3 %shard_map.149 = (bf16[2304,128]{1,0:T(8,128)(2,1)S(1)}, bf16[128,2304]{1,0:T(8,128)(2,1)S(1)}) custom-call(bf16[448,288]{1,0:T(8,128)(2,1)S(1)} %copy.16.res, s32[1,448]{1,0:T(1,128)S(1)} %bitcast.2, bf16[1,288]{1,0:T(2,128)(2,1)S(1)} %reshape.17.gain, bf16[288,288]{1,0:T(8,128)(2,1)S(1)} %copy-done.6, bf16[288,288]{1,0:T(8,128)(2,1)S(1)} %copy-done.7, ...), custom_call_target="tpu_custom_call" | custom-call | tf_op jit(solution)/shard_map/pallas_call | solution.py:468
  142.1 0.8 copy.19
  143.0 0.8 copy.20
  (1 shorter events, 0.0 us)
Async XLA Ops:
  0.6 0.8 copy-start.11
  0.6 2.0 %copy-start = (bf16[2304,128]{1,0:T(8,128)(2,1)S(1)}, bf16[2304,128]{1,0:T(8,128)(2,1)}, u32[]{:S(2)}) copy-start(bf16[2304,128]{1,0:T(8,128)(2,1)} %ew_h.1) | copy-start | bytes 1769476
  1.4 1.2 copy-start.9
  1.4 1.2 copy-start.10
  2.7 1.1 copy-start.1
  3.7 1.1 copy-start.2
  4.8 1.1 copy-start.3
  5.9 1.1 copy-start.4
  6.9 1.1 copy-start.5
  8.0 0.9 copy-start.6
  8.9 0.9 copy-start.7
  9.9 0.9 copy-start.8

commit v2 on v1

v2 whole, which is shorter than its diff:
```python
import functools

import jax
import jax.numpy as jnp
from jax import lax
from jax.experimental import pallas as pl
from jax.experimental.pallas import tpu as pltpu
from jax.sharding import PartitionSpec as P

SPECIAL = 4
TOK = 448
HALF = 224
D = 2304
W = 288
ZN = 16
SRC = 8
FEAT = 64

eps_rms = 1e-06
beta_one = 0.9
beta_two = 0.999
adam_count = 100.0
l1_coeff = 0.2

F32 = jnp.float32
BF16 = jnp.bfloat16


def tiles(v):
    return v.reshape(v.shape[0] // 16, 16, 128)


def rows(v):
    return v.reshape(v.shape[0] * 16, 128)


def dot(a, b, ca=1, cb=0):
    return lax.dot_general(a, b, (((ca,), (cb,)), ((), ())), preferred_element_type=F32)


def lane_group(shape):
    return lax.broadcasted_iota(jnp.int32, shape, len(shape) - 1)


def fold(read, lanes):
    out = read(3)
    for g in (2, 1, 0):
        out = jnp.where(lanes < 32 * (g + 1), read(g), out)
    return out


FAR = (8, 9, 7, 10, 6, 11, 5, 12, 4, 13, 3)
GROUPS = ((3, 5), (12, 14), (5, 7), (10, 12), (7, 10))
GROUP_OF = {place: g for g, (lo, hi) in enumerate(GROUPS) for place in range(lo, hi)}


def adam(grad, first, second, clip):
    corr_one = 1.0 - beta_one**adam_count
    corr_two = 1.0 - beta_two**adam_count
    scaled_grad = clip * grad
    mean = (beta_one / corr_one) * first.astype(F32) + ((1.0 - beta_one) / corr_one) * scaled_grad
    power = (beta_two / corr_two) * second.astype(F32) + ((1.0 - beta_two) / corr_two) * (scaled_grad * scaled_grad)
    return (mean / (jnp.sqrt(power) + 1e-08)).astype(BF16)


def adam_kernel(clip, eg, ef, es, dg, df, ds, eo_h, do_h, eo, do, sem):
    scale = clip[0:1, 0:1]
    copies = []
    for p in range(6):
        at = slice(384 * p, 384 * p + 384)
        do[:, at] = adam(dg[:, at], df[:, at], ds[:, at], scale)
        copies.append(pltpu.make_async_copy(do.at[:, at], do_h.at[:, at], sem.at[2 * p]))
        copies[-1].start()
        eo[at] = adam(eg[at], ef[at], es[at], scale)
        copies.append(pltpu.make_async_copy(eo.at[at], eo_h.at[at], sem.at[2 * p + 1]))
        copies[-1].start()
    for cp in copies:
        cp.wait()


def kernel(
    res_t, tok, gain, gw, uw, dw_h, ew_h, eb, dcw_h, db, ef_h, es_h, df_h, ds_h,
    eg, dg, clip, ef, es, df, ds,
    dw, ew, dcw, ebx,
    rf, rn, rt, gu, p1r, sqs, sqr, hb, hh, dwf, tail, rest, ot, p3r,
    gs, ss, twb, bias, pa, lat_t, tt, p5r, zb, own, aa, p5z, ee, st,
    dgs, dgr, egs, egr, n7, n7z, n7x,
    lsem, wsend, wrecv, ssem, rsem,
):
    s = lax.axis_index("src")
    f = lax.axis_index("feat")
    c = lax.rem(f, 2)
    q = lax.div(f, 2)
    z = lax.rem(q, ZN)
    yhi = lax.div(q, ZN)
    xy = s * 2 + yhi
    half = lax.div(s, 4)

    def to(src, feat):
        return {"device_id": (src, feat), "device_id_type": pl.DeviceIdType.MESH}

    other = to(s, q * 2 + 1 - c)

    def src_peer(d, core):
        return to(lax.rem(s + d, SRC), q * 2 + core)

    def q_peer(d):
        return to(s, lax.rem(q + d, 32) * 2 + c)

    def z_peer(d):
        return to(s, (yhi * ZN + lax.rem(z + d, ZN)) * 2 + c)

    def xy_peer(d, core=c):
        i = lax.rem(xy + d, 16)
        return to(lax.div(i, 2), (lax.rem(i, 2) * ZN + z) * 2 + core)

    def loop(n, fn):
        def body(d, carry):
            fn(d)
            return carry

        lax.fori_loop(1, n, body, 0)

    def send(src, dst, k, where, at=None):
        pltpu.make_async_remote_copy(
            src_ref=src, dst_ref=dst, send_sem=ssem.at[k], recv_sem=rsem.at[k if at is None else at], **where
        ).start()

    def arrived(ref, k):
        pltpu.make_async_copy(ref, ref, rsem.at[k]).wait()

    def left(ref, k):
        pltpu.make_async_copy(ref, ref, ssem.at[k]).wait()

    place_of = [lax.rem(k + ZN - z, ZN) for k in range(ZN)]

    def far_first(n, d):
        step = lax.div(d, 2)
        return n // 2 + jnp.where(lax.rem(d, 2) == 0, step, -step)

    def gather(buf, k, m):
        mine = buf.at[xy, 0]
        for d in FAR:
            send(mine, buf.at[xy, ZN - d], k, z_peer(d), m + GROUP_OF[ZN - d])
        loop(16, lambda d: send(mine, mine, k + 1, xy_peer(d), m + 5))

        def onward(g):
            lo, hi = GROUPS[g]
            arrived(buf.at[0, lo:hi], m + g)
            part = buf.at[xy, lo:hi]
            loop(16, lambda d: send(part, part, k + 1, xy_peer(d), m + 6))

        onward(0)
        onward(1)
        arrived(buf.at[0, 0:15], m + 5)
        for d in (2, 14, 1, 15):
            send(buf.at[:, 0], buf.at[:, ZN - d], k + 2, z_peer(d), m + 7)
        onward(2)
        onward(3)
        onward(4)
        arrived(buf.at[0:15, 0:11], m + 6)
        arrived(buf.at[:, 0:4], m + 7)

    def gathered(buf, k):
        left(buf.at[0, 0:11], k)
        left(buf.at[0:15, 0:12], k + 1)
        left(buf.at[:, 0:4], k + 2)

    barrier = pltpu.get_barrier_semaphore()
    pl.semaphore_signal(barrier, inc=1, **other)

    def greet(d):
        pl.semaphore_signal(barrier, inc=1, **src_peer(d, c))
        pl.semaphore_signal(barrier, inc=1, **src_peer(d, 1 - c))
        for core in (c, 1 - c):
            pl.semaphore_signal(
                barrier, inc=1, **to(lax.rem(s + d, SRC), (lax.rem(yhi + 1, 2) * ZN + z) * 2 + core)
            )

    pl.semaphore_signal(barrier, inc=1, **to(s, (lax.rem(yhi + 1, 2) * ZN + z) * 2 + 1 - c))
    loop(SRC, greet)
    loop(32, lambda d: pl.semaphore_signal(barrier, inc=1, **q_peer(d)))

    loads = []
    for k, (src, dst) in enumerate(
        ((dw_h, dw), (ew_h, ew.at[0]), (dcw_h, dcw.at[0]), (ef_h, ef), (es_h, es), (df_h, df), (ds_h, ds))
    ):
        cp = pltpu.make_async_copy(src, dst, lsem.at[k])
        cp.start()
        loads.append(cp)

    lanes = lane_group((64, 128))
    pick = jnp.where(
        jnp.bitwise_and(lane_group((32, 128)), 31) == lax.broadcasted_iota(jnp.int32, (32, 128), 0), 1.0, 0.0
    ).astype(BF16)

    turned = jnp.concatenate([res_t[...].astype(F32), jnp.zeros((W, 64), F32)], axis=1)
    rf[...] = turned.T
    xg = (rf[0:448] * gain[...].astype(F32).reshape(1, W)).astype(BF16)
    for k, w in enumerate((gw, uw)):
        main = dot(xg, w[:, 0:256])
        spread = dot(w[:, 256:288], pick).astype(BF16)
        tail[0:448] = dot(xg, spread)
        tail[448:512] = jnp.zeros((64, 128), F32)
        for h in range(2):
            for j in range(2):
                gu[k, h * 32 + 14 * j : h * 32 + 14 * j + 14] = tiles(
                    main[224 * h : 224 * h + 224, 128 * j : 128 * j + 128].astype(BF16)
                )
            part = fold(lambda g: tail[224 * h + 64 * g : 224 * h + 64 * g + 64], lanes)
            gu[k, h * 32 + 28 : h * 32 + 32] = tiles(part.astype(BF16))
    squares = jnp.sum(turned * turned, axis=0, keepdims=True)
    sqs[...] = jnp.concatenate(
        [squares[:, 128 * k : 128 * k + 128] for k in range(4)] + [jnp.zeros((4, 128), F32)], axis=0
    )

    pl.semaphore_wait(barrier, 61)

    def send_p1(d):
        t = lax.rem(s + d, SRC)
        send(gu.at[:, pl.ds(8 * t, 8)], p1r.at[d - 1], 0, src_peer(d, c))
        send(sqs, sqr.at[d - 1], 1, src_peer(d, c))

    loop(SRC, send_p1)

    ids = tok[...]
    live = jnp.where(ids >= SPECIAL, 1.0, 0.0)
    weight = live / jnp.maximum(jnp.sum(live), 1.0)
    weight = jnp.concatenate([weight, jnp.zeros((1, 64), F32)], axis=1)
    weight = jnp.concatenate(
        [weight[:, 128 * k : 128 * k + 128] for k in range(4)] + [jnp.zeros((124, 128), F32)], axis=0
    ).T
    for k in range(4):
        twb[128 * k : 128 * k + 128] = jnp.broadcast_to(weight[:, k : k + 1], (128, 128))
    for k in range(18):
        bias[k] = jnp.broadcast_to(db[128 * k : 128 * k + 128].astype(F32).reshape(1, 128), (8, 128))
    ebx[0] = jnp.broadcast_to(eb[...].astype(F32), (8, 128))

    def share(ref, k):
        return pltpu.make_async_remote_copy(
            src_ref=ref.at[0], dst_ref=ref.at[1], send_sem=wsend.at[k], recv_sem=wrecv.at[k], **other
        )

    shares = [share(ebx, 0), share(dwf, 1), share(ew, 2), share(dcw, 3)]
    shares[0].start()
    loads[0].wait()
    spread = dot(dw[:, 256:288], pick).astype(BF16)
    dwf[0, 0:256, 0:256] = dw[0:256, 0:256]
    dwf[0, 0:256, 256:384] = spread[0:256]
    for g in range(4):
        dwf[0, 256 + 32 * g : 288 + 32 * g, 0:256] = dw[256:288, 0:256]
        dwf[0, 256 + 32 * g : 288 + 32 * g, 256:384] = spread[256:288]
    shares[1].start()
    loads[1].wait()
    shares[2].start()
    loads[2].wait()
    shares[3].start()

    off = pl.multiple_of(HALF * c, 32)
    for j in range(2):
        rest[14 * j : 14 * j + 14] = tiles(rf[pl.ds(off, HALF), 128 * j : 128 * j + 128])
    tail[0:448] = dot(rf[0:448, 256:288].astype(BF16), pick)
    tail[448:512] = jnp.zeros((64, 128), F32)
    rest[28:32] = tiles(fold(lambda g: tail[pl.ds(off + 64 * g, 64)], lanes))
    ss[252:256] = jnp.zeros((4, 16, 128), BF16)
    for k in range(12, 16):
        tt[15, place_of[k]] = jnp.zeros((16, 128), BF16)

    arrived(sqr, 1)
    total = sqs[...]
    for d in range(7):
        total = total + sqr[d]
    inv = lax.rsqrt(total / D + eps_rms)
    inv = jnp.concatenate([inv, jnp.zeros((120, 128), F32)], axis=0).T
    for k in range(4):
        rn[128 * k : 128 * k + 128] = jnp.broadcast_to(inv[:, k : k + 1], (128, 128))
    for h in range(2):
        for j in range(2):
            rt[h * 32 + 14 * j : h * 32 + 14 * j + 14] = tiles(rn[224 * h : 224 * h + 224])
        rt[h * 32 + 28 : h * 32 + 32] = tiles(
            fold(lambda g: rn[224 * h + 64 * g : 224 * h + 64 * g + 64], lanes)
        )

    arrived(p1r, 0)
    acts = []
    for k in range(2):
        acc = gu[k, pl.ds(8 * s, 8)].astype(F32)
        for d in range(7):
            acc = acc + p1r[d, k].astype(F32)
        acts.append(acc * rt[pl.ds(8 * s, 8)])
    hb[...] = (jax.nn.gelu(acts[0], approximate=True) * acts[1]).astype(BF16)

    slot = jnp.where(c == half, 0, 1)
    place = hh.at[slot, pl.ds(8 * lax.rem(s, 4), 8)]

    @pl.when(c == half)
    def _():
        pltpu.make_async_copy(hb, place, rsem.at[2]).start()

    @pl.when(c != half)
    def _():
        send(hb, place, 2, src_peer(0, half))

    loop(SRC, lambda d: send(hb, place, 2, src_peer(d, half)))
    shares[1].wait()
    arrived(hh, 2)
    acc = jnp.zeros((HALF, 384), F32)
    for k in range(2):
        last = rows(hh[k, 28:32])
        keep = jnp.zeros_like(last)
        split = jnp.concatenate(
            [jnp.where((lanes >= 32 * g) & (lanes < 32 * g + 32), last, keep) for g in range(4)], axis=0
        )[0:HALF]
        lhs = jnp.concatenate([rows(hh[k, 0:14]), rows(hh[k, 14:28]), split], axis=1)
        acc = acc + dot(lhs, dwf[k])
    for j in range(2):
        ot[14 * j : 14 * j + 14] = tiles(acc[:, 128 * j : 128 * j + 128].astype(BF16))
    tail[0:224] = acc[:, 256:384]
    tail[224:256] = jnp.zeros((32, 128), F32)
    ot[28:32] = tiles(fold(lambda g: tail[64 * g : 64 * g + 64], lanes).astype(BF16))


    def send_p3(d):
        k = far_first(32, d)
        send(ot.at[lax.rem(q + k, 32)], p3r.at[k - 1], 3, q_peer(k))

    loop(32, send_p3)
    arrived(p3r, 3)
    acc = ot[q].astype(F32)
    for d in range(31):
        acc = acc + p3r[d].astype(F32)
    gs[xy, 0] = (rest[q] + acc).astype(BF16)

    gather(gs, 4, 14)

    def picked(buf, first, n):
        return jnp.concatenate([buf[t // 16, place_of[t % 16]] for t in range(first, first + n)], axis=0)

    acc = jnp.zeros((HALF, 128), F32)
    rem = jnp.zeros((64, 128), F32)
    for k in range(SRC):
        for j in range(2):
            v = picked(gs, 32 * k + 14 * j, 14).astype(F32)
            acc = acc + v * v
        v = picked(gs, 32 * k + 28, 4).astype(F32)
        rem = rem + v * v
    acc = acc + jnp.concatenate(
        [jnp.where((lanes >= 32 * g) & (lanes < 32 * g + 32), rem, 0.0) for g in range(4)], axis=0
    )[0:HALF]
    inv = lax.rsqrt(jnp.sum(acc, axis=1, keepdims=True) / D + eps_rms)
    tall = lane_group((HALF, 128))

    def turn(v, by):
        by = by % 128
        return v if by == 0 else pltpu.roll(v, by, 1)

    for k in range(SRC):
        m, base = k % 4, 9 * (k // 4)
        a0 = turn(picked(gs, 32 * k, 14).astype(F32) * inv, 32 * m)
        a1 = turn(picked(gs, 32 * k + 14, 14).astype(F32) * inv, 32 * m)
        last = picked(gs, 32 * k + 28, 4).astype(F32)
        rem = jnp.concatenate([turn(last, 32 * m - 32 * g) for g in range(4)], axis=0)[0:HALF] * inv
        if m == 0:
            first, second = a0, a1
        else:
            first = jnp.where(tall < 32 * m, carry, a0)
            second = jnp.where(tall < 32 * m, a0, a1)
        carry = jnp.where(tall < 32 * m, a1, rem)
        for at, v in ((2 * m, first), (2 * m + 1, second)) + (((8, carry),) if m == 3 else ()):
            ss[14 * (base + at) : 14 * (base + at) + 14] = tiles(v.astype(BF16))

    def cols_of(ref, p):
        return jnp.concatenate([rows(ref[28 * p : 28 * p + 14]), rows(ref[28 * p + 14 : 28 * p + 28])], axis=1)

    for k in (0, 2, 3):
        shares[k].wait()
    acc = jnp.zeros((HALF, 256), F32)
    for p in range(9):
        rhs = jnp.concatenate([ew[0, 256 * p : 256 * p + 256], ew[1, 256 * p : 256 * p + 256]], axis=1)
        acc = acc + dot(cols_of(ss, p), rhs)
    acc = acc + jnp.concatenate([ebx[0, 0:1], ebx[1, 0:1]], axis=1)
    pa[...] = acc
    latents = jnp.maximum(acc, 0.0)
    lat = latents.astype(BF16)
    for p in range(9):
        rhs = jnp.concatenate([dcw[0, :, 256 * p : 256 * p + 256], dcw[1, :, 256 * p : 256 * p + 256]], axis=0)
        r = dot(lat, rhs).astype(BF16)
        for t in range(28 * p, 28 * p + 28):
            k = t - 28 * p
            tt[t // 16, place_of[t % 16]] = r[16 * (k % 14) : 16 * (k % 14) + 16, 128 * (k // 14) : 128 * (k // 14) + 128]

    def across(g):
        lo, hi = GROUPS[g]
        loop(
            16,
            lambda d: send(
                tt.at[lax.rem(xy + d, 16), lo:hi], p5r.at[d - 1, lo:hi], 7, xy_peer(d), 22 + g
            ),
        )

    across(4)
    for k, d in enumerate((2, 14, 1, 15)):
        send(tt.at[:, d], zb.at[k], 8, z_peer(d), 28)
    for g in (2, 3, 0, 1):
        across(g)
    lat_t[...] = jnp.concatenate([latents, jnp.zeros((32, 256), F32)], axis=0).T.astype(BF16)
    for p in range(18):
        v = rows(ss[14 * p : 14 * p + 14]).astype(F32)
        st[128 * p : 128 * p + 128] = jnp.concatenate([v, jnp.zeros((32, 128), F32)], axis=0).T.astype(BF16)

    def onward(g):
        lo, hi = GROUPS[g]
        arrived(p5r.at[:, lo:hi], 22 + g)
        for k in range(lo, hi):
            acc = tt[xy, k].astype(F32)
            for d in range(15):
                acc = acc + p5r[d, k].astype(F32)
            aa[k] = acc.astype(BF16)
            send(aa.at[k], p5z.at[k - 3], 9, z_peer(k), 29)

    onward(4)
    arrived(zb, 28)
    for k in range(16):
        acc = tt[k, 0].astype(F32)
        for d in range(4):
            acc = acc + zb[d, k].astype(F32)
        own[k] = acc.astype(BF16)
    loop(16, lambda d: send(own.at[lax.rem(xy + d, 16)], p5r.at[d - 1, 0], 7, xy_peer(d), 27))
    for g in (2, 3, 0, 1):
        onward(g)
    arrived(p5r.at[:, 0], 27)
    acc = own[xy].astype(F32)
    for d in range(15):
        acc = acc + p5r[d, 0].astype(F32)
    arrived(p5z, 29)
    for d in range(11):
        acc = acc + p5z[d].astype(F32)
    t = xy * 16 + z
    col = jnp.minimum(lax.div(t, 14), 17)
    row = lax.rem(t, 14)
    err = (acc + bias[col, 0:1] - ss[t].astype(F32)).astype(BF16)
    tw = twb[pl.ds(pl.multiple_of(off + 16 * row, 16), 16)]
    ee[xy, 0] = (2.0 * tw * err.astype(F32)).astype(BF16)
    gather(ee, 10, 30)

    def err_cols(p):
        return jnp.concatenate([picked(ee, 28 * p, 14), picked(ee, 28 * p + 14, 14)], axis=1)

    acc = jnp.zeros((HALF, 256), F32)
    for p in range(9):
        rhs = jnp.concatenate([dcw[0, :, 256 * p : 256 * p + 256], dcw[1, :, 256 * p : 256 * p + 256]], axis=0)
        acc = acc + dot(err_cols(p), rhs, 1, 1)
    tw = l1_coeff * twb[pl.ds(off, HALF)]
    acc = acc + jnp.concatenate([tw, tw], axis=1)
    pg = jnp.where(pa[...] > 0.0, acc, 0.0).astype(BF16)
    for p in range(9):
        r = dot(st[256 * p : 256 * p + 256, 0:HALF], pg)
        eg[256 * p : 256 * p + 256] = r[:, 0:128]
        egs[256 * p : 256 * p + 256] = r[:, 128:256].astype(BF16)
        if p % 3 == 2:
            part = pl.ds(768 * (p // 3), 768)
            send(egs.at[part], egr.at[part], 13, other, 38 + p // 3)
    lt = lat_t[:, 0:HALF]
    for p in range(9):
        r = dot(lt, err_cols(p))
        dg[:, 256 * p : 256 * p + 256] = r[0:128]
        dgs[:, 256 * p : 256 * p + 256] = r[128:256].astype(BF16)
        if p % 3 == 2:
            part = pl.ds(768 * (p // 3), 768)
            send(dgs.at[:, part], dgr.at[:, part], 14, other, 41 + p // 3)
    acc = jnp.zeros((8, 128), F32)
    for p in range(18):
        if p % 6 == 0:
            arrived(egr.at[0:768], 38 + p // 6)
        v = eg[128 * p : 128 * p + 128] + egr[128 * p : 128 * p + 128].astype(F32)
        eg[128 * p : 128 * p + 128] = v
        acc = acc + jnp.sum((v * v).reshape(16, 8, 128), axis=0)
    for p in range(18):
        if p % 6 == 0:
            arrived(dgr.at[:, 0:768], 41 + p // 6)
        v = dg[:, 128 * p : 128 * p + 128] + dgr[:, 128 * p : 128 * p + 128].astype(F32)
        dg[:, 128 * p : 128 * p + 128] = v
        acc = acc + jnp.sum((v * v).reshape(16, 8, 128), axis=0)

    n7[0] = acc

    def send_n(d):
        k = far_first(ZN, d)
        send(n7.at[0], n7z.at[k - 1], 15, z_peer(k), 44)

    loop(ZN, send_n)
    arrived(n7z, 44)
    for d in range(15):
        acc = acc + n7z[d]
    n7[1] = acc

    def send_xy(d):
        send(n7.at[1], n7x.at[d - 1], 16, xy_peer(d), 45)
        send(n7.at[1], n7x.at[d + 15], 16, xy_peer(d, 1 - c), 45)

    loop(16, send_xy)
    send(n7.at[1], n7x.at[15], 16, other, 45)
    arrived(n7x, 45)
    for d in range(31):
        acc = acc + n7x[d]
    clip[...] = jnp.broadcast_to(lax.rsqrt(jnp.sum(acc, keepdims=True) + 1e-12), (8, 128))
    for k in range(3, 7):
        loads[k].wait()

    left(p1r, 0)
    left(sqr, 1)

    @pl.when(c == half)
    def _():
        left(hh.at[0, 0:28], 2)
        left(hh.at[1, 0:28], 2)

    @pl.when(c != half)
    def _():
        left(hh, 2)

    left(p3r, 3)
    gathered(gs, 4)
    left(p5r.at[:, 0:12], 7)
    left(zb, 8)
    left(p5z, 9)
    gathered(ee, 10)
    left(egs, 13)
    left(dgs, 14)
    left(n7z, 15)
    left(n7x, 16)


def local(
    residual, token_ids, ffn_gain, gate_w, up_w, down_w, enc_w, enc_bias, dec_w, dec_bias,
    enc_first, enc_second, dec_first, dec_second,
):
    vm = pl.BlockSpec(memory_space=pltpu.VMEM)
    hbm = pl.BlockSpec(memory_space=pl.ANY)
    V = pltpu.VMEM
    scratch = [
        V((W, W), BF16), V((2, D, 128), BF16), V((2, 128, D), BF16), V((2, 8, 128), F32),
        V((512, W), F32), V((512, 128), F32), V((64, 16, 128), F32), V((2, 64, 16, 128), BF16),
        V((7, 2, 8, 16, 128), BF16), V((8, 128), F32), V((7, 8, 128), F32), V((8, 16, 128), BF16),
        V((2, 32, 16, 128), BF16), V((2, 384, 384), BF16), V((512, 128), F32), V((32, 16, 128), F32),
        V((32, 16, 128), BF16), V((31, 16, 128), BF16),
        V((16, 16, 16, 128), BF16), V((256, 16, 128), BF16), V((512, 128), F32), V((18, 8, 128), F32),
        V((HALF, 256), F32), V((256, 256), BF16), V((16, 16, 16, 128), BF16), V((15, 16, 16, 128), BF16),
        V((4, 16, 16, 128), BF16), V((16, 16, 128), BF16), V((16, 16, 128), BF16), V((11, 16, 128), BF16),
        V((16, 16, 16, 128), BF16), V((D, 256), BF16),
        V((128, D), BF16), V((128, D), BF16), V((D, 128), BF16), V((D, 128), BF16),
        V((2, 8, 128), F32), V((15, 8, 128), F32), V((31, 8, 128), F32),
        pltpu.SemaphoreType.DMA((7,)), pltpu.SemaphoreType.DMA((4,)), pltpu.SemaphoreType.DMA((4,)),
        pltpu.SemaphoreType.DMA((17,)), pltpu.SemaphoreType.DMA((46,)),
    ]
    operands = [
        pltpu.with_memory_space_constraint(v, pltpu.HBM)
        for v in (
            residual.T, token_ids.reshape(1, TOK), ffn_gain, gate_w, up_w, down_w, enc_w,
            enc_bias.reshape(1, 128), dec_w, dec_bias, enc_first, enc_second, dec_first, dec_second,
        )
    ]
    tall, flat = jax.ShapeDtypeStruct((D, 128), BF16), jax.ShapeDtypeStruct((128, D), BF16)
    enc_grad, dec_grad, clip, enc_one, enc_two, dec_one, dec_two = pl.pallas_call(
        kernel,
        out_shape=(
            jax.ShapeDtypeStruct((D, 128), F32),
            jax.ShapeDtypeStruct((128, D), F32),
            jax.ShapeDtypeStruct((8, 128), F32),
            tall, tall, flat, flat,
        ),
        in_specs=[vm, vm, vm, vm, vm, hbm, hbm, vm, hbm, vm, hbm, hbm, hbm, hbm],
        out_specs=(vm,) * 7,
        scratch_shapes=scratch,
        compiler_params=pltpu.CompilerParams(
            collective_id=0, has_side_effects=True, vmem_limit_bytes=32 << 20
        ),
    )(*operands)
    return pl.pallas_call(
        adam_kernel,
        out_shape=(tall, flat),
        in_specs=[vm] * 7,
        out_specs=(hbm, hbm),
        scratch_shapes=[V((D, 128), BF16), V((128, D), BF16), pltpu.SemaphoreType.DMA((12,))],
        compiler_params=pltpu.CompilerParams(vmem_limit_bytes=16 << 20),
    )(clip, enc_grad, enc_one, enc_two, dec_grad, dec_one, dec_two)


def solution(mesh):
    in_specs = (
        P(None, "src"),
        P(),
        P("src"),
        P("src", "feat"),
        P("src", "feat"),
        P("feat", "src"),
        P(None, ("src", "feat")),
        P(("src", "feat")),
        P(("src", "feat"), None),
        P(),
        P(None, ("src", "feat")),
        P(None, ("src", "feat")),
        P(("src", "feat"), None),
        P(("src", "feat"), None),
    )
    out_specs = (P(None, ("src", "feat")), P(("src", "feat"), None))
    return jax.shard_map(local, mesh=mesh, in_specs=in_specs, out_specs=out_specs, check_vma=False)
```

time: 144 us -> 112 us (0.78)
  Pallas kernels: 131 us -> 111 us
  local copies, waits for them, and re-layouts: 11.7 us -> 0 us
    pallas_call x1 -> x2, Pallas kernels: 131 us -> 111 us  [the longest x1 109 us: local(): pl.pallas_call(kernel, out_shape=(jax.ShapeDtypeStruct((D, 128), F32), ja...]
    unnamed x27 -> x0, local copies, waits for them, and re-layouts: 11 us -> none
where the time goes in v2:
time: 112 us
  Pallas kernels  111 us (99%)
    pallas_call x1, Pallas kernels, local(): pl.pallas_call(kernel, out_shape=(jax.ShapeDtypeStruct((D, 128), F32), ja...  109 us
    pallas_call x1, Pallas kernels, local(): pl.pallas_call(adam_kernel, out_shape=(tall, flat), in_specs=[vm] * 7, ou...  2.56 us

profile of v2, /device:TPU:1, one launch (start us, length us, event | category | flops | bytes accessed | tf_op | source)
XLA Modules:
  0.0 112.1 jit_solution(2163895215436424765)
XLA Ops:
  0.6 108.8 %shard_map.149 = (f32[2304,128]{1,0:T(8,128)S(1)}, f32[128,2304]{1,0:T(8,128)S(1)}, f32[8,128]{1,0:T(8,128)S(1)}, bf16[2304,128]{1,0:T(8,128)(2,1)S(1)}, bf16[23...) custom-call(bf16[288,448]{1,0:T(8,128)(2,1)} %bitcast.3, s32[1,448]{1,0:T(1,128)} %bitcast.4, ...), custom_call_target="tpu_custom_call" | custom-call | tf_op jit(solution)/shard_map/pallas_call | solution.py:564
  109.5 2.6 %shard_map.150 = (bf16[2304,128]{1,0:T(8,128)(2,1)}, bf16[128,2304]{1,0:T(8,128)(2,1)}) custom-call(f32[8,128]{1,0:T(8,128)S(1)} %get-tuple-element.9.clip, f32[2304,128]{1,0:T(8,128)S(1)} %get-tuple-element.10.eg, bf16[2304,128]{1,0:T(8,128)(2,1)S(1)} %get-tuple-element.11.ef, bf16[2304,128]{1,0:T(8,128)(2,1)S(1)} %get-tuple-element.12.es, ...), custom_call_target="tpu_custom_call" | custom-call | tf_op jit(solution)/shard_map/pallas_call | solution.py:579

commit v3 on v2

--- a/solution.py
+++ b/solution.py
@@ -50,7 +50,7 @@
 
 
 FAR = (8, 9, 7, 10, 6, 11, 5, 12, 4, 13, 3)
-GROUPS = ((3, 5), (12, 14), (5, 7), (10, 12), (7, 10))
+GROUPS = ((3, 5), (12, 14), (5, 7), (10, 12), (7, 8), (9, 10), (8, 9))
 GROUP_OF = {place: g for g, (lo, hi) in enumerate(GROUPS) for place in range(lo, hi)}
 
 
@@ -79,9 +79,9 @@
 
 
 def kernel(
-    res_t, tok, gain, gw, uw, dw_h, ew_h, eb, dcw_h, db, ef_h, es_h, df_h, ds_h,
+    res_h, tok_h, gain_h, gw_h, uw_h, dw_h, ew_h, eb_h, dcw_h, db_h, ef_h, es_h, df_h, ds_h,
     eg, dg, clip, ef, es, df, ds,
-    dw, ew, dcw, ebx,
+    res_t, gain, gw, uw, tok, eb, db, dw, ew, dcw, ebx,
     rf, rn, rt, gu, p1r, sqs, sqr, hb, hh, dwf, tail, rest, ot, p3r,
     gs, ss, twb, bias, pa, lat_t, tt, p5r, zb, own, aa, p5z, ee, st,
     dgs, dgr, egs, egr, n7, n7z, n7x,
@@ -142,44 +142,58 @@
         mine = buf.at[xy, 0]
         for d in FAR:
             send(mine, buf.at[xy, ZN - d], k, z_peer(d), m + GROUP_OF[ZN - d])
-        loop(16, lambda d: send(mine, mine, k + 1, xy_peer(d), m + 5))
+        loop(16, lambda d: send(mine, mine, k + 1, xy_peer(d), m + 7))
 
         def onward(g):
             lo, hi = GROUPS[g]
             arrived(buf.at[0, lo:hi], m + g)
             part = buf.at[xy, lo:hi]
-            loop(16, lambda d: send(part, part, k + 1, xy_peer(d), m + 6))
+            loop(16, lambda d: send(part, part, k + 1, xy_peer(d), m + 8))
 
         onward(0)
         onward(1)
-        arrived(buf.at[0, 0:15], m + 5)
+        arrived(buf.at[0, 0:15], m + 7)
         for d in (2, 14, 1, 15):
-            send(buf.at[:, 0], buf.at[:, ZN - d], k + 2, z_peer(d), m + 7)
+            send(buf.at[:, 0], buf.at[:, ZN - d], k + 2, z_peer(d), m + 9)
         onward(2)
-        onward(3)
-        onward(4)
-        arrived(buf.at[0:15, 0:11], m + 6)
-        arrived(buf.at[:, 0:4], m + 7)
+        for g in (3, 4, 5, 6):
+            onward(g)
+        arrived(buf.at[0:15, 0:11], m + 8)
+        arrived(buf.at[:, 0:4], m + 9)
 
     def gathered(buf, k):
         left(buf.at[0, 0:11], k)
         left(buf.at[0:15, 0:12], k + 1)
         left(buf.at[:, 0:4], k + 2)
 
+    fetched = []
+    for k, (src, dst) in enumerate(((res_h, res_t), (gain_h, gain), (gw_h, gw), (uw_h, uw), (tok_h, tok), (eb_h, eb), (db_h, db))):
+        cp = pltpu.make_async_copy(src, dst, lsem.at[7 + k])
+        cp.start()
+        fetched.append(cp)
+
     barrier = pltpu.get_barrier_semaphore()
-    pl.semaphore_signal(barrier, inc=1, **other)
-
-    def greet(d):
-        pl.semaphore_signal(barrier, inc=1, **src_peer(d, c))
-        pl.semaphore_signal(barrier, inc=1, **src_peer(d, 1 - c))
+
+    def greet(where):
+        pl.semaphore_signal(barrier, inc=1, **where)
+
+    def greet_z(d):
+        k = far_first(ZN, d)
+        greet(q_peer(k))
+        greet(q_peer(k + 16))
+
+    def greet_src(d):
+        k = far_first(SRC, d)
+        greet(src_peer(k, c))
+        greet(src_peer(k, 1 - c))
         for core in (c, 1 - c):
-            pl.semaphore_signal(
-                barrier, inc=1, **to(lax.rem(s + d, SRC), (lax.rem(yhi + 1, 2) * ZN + z) * 2 + core)
-            )
-
-    pl.semaphore_signal(barrier, inc=1, **to(s, (lax.rem(yhi + 1, 2) * ZN + z) * 2 + 1 - c))
-    loop(SRC, greet)
-    loop(32, lambda d: pl.semaphore_signal(barrier, inc=1, **q_peer(d)))
+            greet(to(lax.rem(s + k, SRC), (lax.rem(yhi + 1, 2) * ZN + z) * 2 + core))
+
+    loop(ZN, greet_z)
+    loop(SRC, greet_src)
+    greet(q_peer(16))
+    greet(other)
+    greet(to(s, (lax.rem(yhi + 1, 2) * ZN + z) * 2 + 1 - c))
 
     loads = []
     for k, (src, dst) in enumerate(
@@ -194,22 +208,29 @@
         jnp.bitwise_and(lane_group((32, 128)), 31) == lax.broadcasted_iota(jnp.int32, (32, 128), 0), 1.0, 0.0
     ).astype(BF16)
 
-    turned = jnp.concatenate([res_t[...].astype(F32), jnp.zeros((W, 64), F32)], axis=1)
-    rf[...] = turned.T
-    xg = (rf[0:448] * gain[...].astype(F32).reshape(1, W)).astype(BF16)
+    tail[448:512] = jnp.zeros((64, 256), F32)
+    fetched[0].wait()
+    fetched[1].wait()
+    rf[...] = jnp.concatenate([res_t[...], jnp.zeros((W, 64), BF16)], axis=1).T
+    xg = (rf[0:448].astype(F32) * gain[...].astype(F32).reshape(1, W)).astype(BF16)
+    fetched[2].wait()
+    fetched[3].wait()
+    spread = dot(jnp.concatenate([gw[:, 256:288], uw[:, 256:288]], axis=0), pick).astype(BF16)
+    tail[0:448] = dot(xg, jnp.concatenate([spread[0:W], spread[W : 2 * W]], axis=1))
     for k, w in enumerate((gw, uw)):
         main = dot(xg, w[:, 0:256])
-        spread = dot(w[:, 256:288], pick).astype(BF16)
-        tail[0:448] = dot(xg, spread)
-        tail[448:512] = jnp.zeros((64, 128), F32)
         for h in range(2):
             for j in range(2):
                 gu[k, h * 32 + 14 * j : h * 32 + 14 * j + 14] = tiles(
                     main[224 * h : 224 * h + 224, 128 * j : 128 * j + 128].astype(BF16)
                 )
-            part = fold(lambda g: tail[224 * h + 64 * g : 224 * h + 64 * g + 64], lanes)
+            part = fold(
+                lambda g: tail[224 * h + 64 * g : 224 * h + 64 * g + 64, 128 * k : 128 * k + 128], lanes
+            )
             gu[k, h * 32 + 28 : h * 32 + 32] = tiles(part.astype(BF16))
-    squares = jnp.sum(turned * turned, axis=0, keepdims=True)
+    wide = res_t[...].astype(F32)
+    squares = jnp.sum(wide * wide, axis=0, keepdims=True)
+    squares = jnp.concatenate([squares, jnp.zeros((1, 64), F32)], axis=1)
     sqs[...] = jnp.concatenate(
         [squares[:, 128 * k : 128 * k + 128] for k in range(4)] + [jnp.zeros((4, 128), F32)], axis=0
     )
@@ -217,12 +238,14 @@
     pl.semaphore_wait(barrier, 61)
 
     def send_p1(d):
-        t = lax.rem(s + d, SRC)
-        send(gu.at[:, pl.ds(8 * t, 8)], p1r.at[d - 1], 0, src_peer(d, c))
-        send(sqs, sqr.at[d - 1], 1, src_peer(d, c))
+        k = far_first(SRC, d)
+        send(sqs, sqr.at[k - 1], 1, src_peer(k, c))
+        send(gu.at[:, pl.ds(8 * lax.rem(s + k, SRC), 8)], p1r.at[k - 1], 0, src_peer(k, c))
 
     loop(SRC, send_p1)
 
+    for k in (4, 5, 6):
+        fetched[k].wait()
     ids = tok[...]
     live = jnp.where(ids >= SPECIAL, 1.0, 0.0)
     weight = live / jnp.maximum(jnp.sum(live), 1.0)
@@ -258,10 +281,9 @@
 
     off = pl.multiple_of(HALF * c, 32)
     for j in range(2):
-        rest[14 * j : 14 * j + 14] = tiles(rf[pl.ds(off, HALF), 128 * j : 128 * j + 128])
-    tail[0:448] = dot(rf[0:448, 256:288].astype(BF16), pick)
-    tail[448:512] = jnp.zeros((64, 128), F32)
-    rest[28:32] = tiles(fold(lambda g: tail[pl.ds(off + 64 * g, 64)], lanes))
+        rest[14 * j : 14 * j + 14] = tiles(rf[pl.ds(off, HALF), 128 * j : 128 * j + 128].astype(F32))
+    tail[:, 0:128] = dot(rf[:, 256:288], pick)
+    rest[28:32] = tiles(fold(lambda g: tail[pl.ds(off + 64 * g, 64), 0:128], lanes))
     ss[252:256] = jnp.zeros((4, 16, 128), BF16)
     for k in range(12, 16):
         tt[15, place_of[k]] = jnp.zeros((16, 128), BF16)
@@ -315,16 +337,17 @@
         acc = acc + dot(lhs, dwf[k])
     for j in range(2):
         ot[14 * j : 14 * j + 14] = tiles(acc[:, 128 * j : 128 * j + 128].astype(BF16))
-    tail[0:224] = acc[:, 256:384]
-    tail[224:256] = jnp.zeros((32, 128), F32)
-    ot[28:32] = tiles(fold(lambda g: tail[64 * g : 64 * g + 64], lanes).astype(BF16))
+    tail[0:224, 0:128] = acc[:, 256:384]
+    ot[28:32] = tiles(fold(lambda g: tail[64 * g : 64 * g + 64, 0:128], lanes).astype(BF16))
 
 
     def send_p3(d):
-        k = far_first(32, d)
+        k = far_first(ZN, d)
         send(ot.at[lax.rem(q + k, 32)], p3r.at[k - 1], 3, q_peer(k))
-
-    loop(32, send_p3)
+        send(ot.at[lax.rem(q + k + 16, 32)], p3r.at[k + 15], 3, q_peer(k + 16))
+
+    loop(ZN, send_p3)
+    send(ot.at[lax.rem(q + 16, 32)], p3r.at[15], 3, q_peer(16))
     arrived(p3r, 3)
     acc = ot[q].astype(F32)
     for d in range(31):
@@ -394,13 +417,14 @@
         loop(
             16,
             lambda d: send(
-                tt.at[lax.rem(xy + d, 16), lo:hi], p5r.at[d - 1, lo:hi], 7, xy_peer(d), 22 + g
+                tt.at[lax.rem(xy + d, 16), lo:hi], p5r.at[d - 1, lo:hi], 7, xy_peer(d), 24 + g
             ),
         )
 
-    across(4)
+    for g in (6, 4, 5):
+        across(g)
     for k, d in enumerate((2, 14, 1, 15)):
-        send(tt.at[:, d], zb.at[k], 8, z_peer(d), 28)
+        send(tt.at[:, d], zb.at[k], 8, z_peer(d), 31)
     for g in (2, 3, 0, 1):
         across(g)
     lat_t[...] = jnp.concatenate([latents, jnp.zeros((32, 256), F32)], axis=0).T.astype(BF16)
@@ -410,29 +434,30 @@
 
     def onward(g):
         lo, hi = GROUPS[g]
-        arrived(p5r.at[:, lo:hi], 22 + g)
+        arrived(p5r.at[:, lo:hi], 24 + g)
         for k in range(lo, hi):
             acc = tt[xy, k].astype(F32)
             for d in range(15):
                 acc = acc + p5r[d, k].astype(F32)
             aa[k] = acc.astype(BF16)
-            send(aa.at[k], p5z.at[k - 3], 9, z_peer(k), 29)
-
-    onward(4)
-    arrived(zb, 28)
+            send(aa.at[k], p5z.at[k - 3], 9, z_peer(k), 33)
+
+    for g in (6, 4, 5):
+        onward(g)
+    arrived(zb, 31)
     for k in range(16):
         acc = tt[k, 0].astype(F32)
         for d in range(4):
             acc = acc + zb[d, k].astype(F32)
         own[k] = acc.astype(BF16)
-    loop(16, lambda d: send(own.at[lax.rem(xy + d, 16)], p5r.at[d - 1, 0], 7, xy_peer(d), 27))
+    loop(16, lambda d: send(own.at[lax.rem(xy + d, 16)], p5r.at[d - 1, 0], 7, xy_peer(d), 32))
     for g in (2, 3, 0, 1):
         onward(g)
-    arrived(p5r.at[:, 0], 27)
+    arrived(p5r.at[:, 0], 32)
     acc = own[xy].astype(F32)
     for d in range(15):
         acc = acc + p5r[d, 0].astype(F32)
-    arrived(p5z, 29)
+    arrived(p5z, 33)
     for d in range(11):
         acc = acc + p5z[d].astype(F32)
     t = xy * 16 + z
@@ -441,7 +466,7 @@
     err = (acc + bias[col, 0:1] - ss[t].astype(F32)).astype(BF16)
     tw = twb[pl.ds(pl.multiple_of(off + 16 * row, 16), 16)]
     ee[xy, 0] = (2.0 * tw * err.astype(F32)).astype(BF16)
-    gather(ee, 10, 30)
+    gather(ee, 10, 34)
 
     def err_cols(p):
         return jnp.concatenate([picked(ee, 28 * p, 14), picked(ee, 28 * p + 14, 14)], axis=1)
@@ -459,7 +484,7 @@
         egs[256 * p : 256 * p + 256] = r[:, 128:256].astype(BF16)
         if p % 3 == 2:
             part = pl.ds(768 * (p // 3), 768)
-            send(egs.at[part], egr.at[part], 13, other, 38 + p // 3)
+            send(egs.at[part], egr.at[part], 13, other, 44 + p // 3)
     lt = lat_t[:, 0:HALF]
     for p in range(9):
         r = dot(lt, err_cols(p))
@@ -467,17 +492,17 @@
         dgs[:, 256 * p : 256 * p + 256] = r[128:256].astype(BF16)
         if p % 3 == 2:
             part = pl.ds(768 * (p // 3), 768)
-            send(dgs.at[:, part], dgr.at[:, part], 14, other, 41 + p // 3)
+            send(dgs.at[:, part], dgr.at[:, part], 14, other, 47 + p // 3)
     acc = jnp.zeros((8, 128), F32)
     for p in range(18):
         if p % 6 == 0:
-            arrived(egr.at[0:768], 38 + p // 6)
+            arrived(egr.at[0:768], 44 + p // 6)
         v = eg[128 * p : 128 * p + 128] + egr[128 * p : 128 * p + 128].astype(F32)
         eg[128 * p : 128 * p + 128] = v
         acc = acc + jnp.sum((v * v).reshape(16, 8, 128), axis=0)
     for p in range(18):
         if p % 6 == 0:
-            arrived(dgr.at[:, 0:768], 41 + p // 6)
+            arrived(dgr.at[:, 0:768], 47 + p // 6)
         v = dg[:, 128 * p : 128 * p + 128] + dgr[:, 128 * p : 128 * p + 128].astype(F32)
         dg[:, 128 * p : 128 * p + 128] = v
         acc = acc + jnp.sum((v * v).reshape(16, 8, 128), axis=0)
@@ -486,21 +511,21 @@
 
     def send_n(d):
         k = far_first(ZN, d)
-        send(n7.at[0], n7z.at[k - 1], 15, z_peer(k), 44)
+        send(n7.at[0], n7z.at[k - 1], 15, z_peer(k), 50)
 
     loop(ZN, send_n)
-    arrived(n7z, 44)
+    arrived(n7z, 50)
     for d in range(15):
         acc = acc + n7z[d]
     n7[1] = acc
 
     def send_xy(d):
-        send(n7.at[1], n7x.at[d - 1], 16, xy_peer(d), 45)
-        send(n7.at[1], n7x.at[d + 15], 16, xy_peer(d, 1 - c), 45)
+        send(n7.at[1], n7x.at[d - 1], 16, xy_peer(d), 51)
+        send(n7.at[1], n7x.at[d + 15], 16, xy_peer(d, 1 - c), 51)
 
     loop(16, send_xy)
-    send(n7.at[1], n7x.at[15], 16, other, 45)
-    arrived(n7x, 45)
+    send(n7.at[1], n7x.at[15], 16, other, 51)
+    arrived(n7x, 51)
     for d in range(31):
         acc = acc + n7x[d]
     clip[...] = jnp.broadcast_to(lax.rsqrt(jnp.sum(acc, keepdims=True) + 1e-12), (8, 128))
@@ -539,10 +564,11 @@
     hbm = pl.BlockSpec(memory_space=pl.ANY)
     V = pltpu.VMEM
     scratch = [
-        V((W, W), BF16), V((2, D, 128), BF16), V((2, 128, D), BF16), V((2, 8, 128), F32),
-        V((512, W), F32), V((512, 128), F32), V((64, 16, 128), F32), V((2, 64, 16, 128), BF16),
+        V((W, TOK), BF16), V((W,), BF16), V((W, W), BF16), V((W, W), BF16), V((1, TOK), jnp.int32),
+        V((1, 128), BF16), V((D,), BF16), V((W, W), BF16), V((2, D, 128), BF16), V((2, 128, D), BF16), V((2, 8, 128), F32),
+        V((512, W), BF16), V((512, 128), F32), V((64, 16, 128), F32), V((2, 64, 16, 128), BF16),
         V((7, 2, 8, 16, 128), BF16), V((8, 128), F32), V((7, 8, 128), F32), V((8, 16, 128), BF16),
-        V((2, 32, 16, 128), BF16), V((2, 384, 384), BF16), V((512, 128), F32), V((32, 16, 128), F32),
+        V((2, 32, 16, 128), BF16), V((2, 384, 384), BF16), V((512, 256), F32), V((32, 16, 128), F32),
         V((32, 16, 128), BF16), V((31, 16, 128), BF16),
         V((16, 16, 16, 128), BF16), V((256, 16, 128), BF16), V((512, 128), F32), V((18, 8, 128), F32),
         V((HALF, 256), F32), V((256, 256), BF16), V((16, 16, 16, 128), BF16), V((15, 16, 16, 128), BF16),
@@ -550,8 +576,8 @@
         V((16, 16, 16, 128), BF16), V((D, 256), BF16),
         V((128, D), BF16), V((128, D), BF16), V((D, 128), BF16), V((D, 128), BF16),
         V((2, 8, 128), F32), V((15, 8, 128), F32), V((31, 8, 128), F32),
-        pltpu.SemaphoreType.DMA((7,)), pltpu.SemaphoreType.DMA((4,)), pltpu.SemaphoreType.DMA((4,)),
-        pltpu.SemaphoreType.DMA((17,)), pltpu.SemaphoreType.DMA((46,)),
+        pltpu.SemaphoreType.DMA((14,)), pltpu.SemaphoreType.DMA((4,)), pltpu.SemaphoreType.DMA((4,)),
+        pltpu.SemaphoreType.DMA((17,)), pltpu.SemaphoreType.DMA((52,)),
     ]
     operands = [
         pltpu.with_memory_space_constraint(v, pltpu.HBM)
@@ -569,7 +595,7 @@
             jax.ShapeDtypeStruct((8, 128), F32),
             tall, tall, flat, flat,
         ),
-        in_specs=[vm, vm, vm, vm, vm, hbm, hbm, vm, hbm, vm, hbm, hbm, hbm, hbm],
+        in_specs=[hbm] * 14,
         out_specs=(vm,) * 7,
         scratch_shapes=scratch,
         compiler_params=pltpu.CompilerParams(

time: 112 us -> 110 us (0.982)
    pallas_call x1, Pallas kernels: 109 us -> 107 us  [local(): pl.pallas_call(kernel, out_shape=(jax.ShapeDtypeStruct((D, 128), F32), ja...]
where the time goes in v3:
time: 110 us
  Pallas kernels  110 us (100%)
    pallas_call x1, Pallas kernels, local(): pl.pallas_call(kernel, out_shape=(jax.ShapeDtypeStruct((D, 128), F32), ja...  107 us
    pallas_call x1, Pallas kernels, local(): pl.pallas_call(adam_kernel, out_shape=(tall, flat), in_specs=[vm] * 7, ou...  2.56 us

profile of v3, /device:TPU:1, one launch (start us, length us, event | category | flops | bytes accessed | tf_op | source)
XLA Modules:
  0.0 110.2 jit_solution(8823386923744403224)
XLA Ops:
  0.6 106.9 %shard_map.149 = (f32[2304,128]{1,0:T(8,128)S(1)}, f32[128,2304]{1,0:T(8,128)S(1)}, f32[8,128]{1,0:T(8,128)S(1)}, bf16[2304,128]{1,0:T(8,128)(2,1)S(1)}, bf16[23...) custom-call(bf16[288,448]{1,0:T(8,128)(2,1)} %bitcast.3, s32[1,448]{1,0:T(1,128)} %bitcast.4, ...), custom_call_target="tpu_custom_call" | custom-call | tf_op jit(solution)/shard_map/pallas_call | solution.py:590
  107.6 2.6 %shard_map.150 = (bf16[2304,128]{1,0:T(8,128)(2,1)}, bf16[128,2304]{1,0:T(8,128)(2,1)}) custom-call(f32[8,128]{1,0:T(8,128)S(1)} %get-tuple-element.9.clip, f32[2304,128]{1,0:T(8,128)S(1)} %get-tuple-element.10.eg, bf16[2304,128]{1,0:T(8,128)(2,1)S(1)} %get-tuple-element.11.ef, bf16[2304,128]{1,0:T(8,128)(2,1)S(1)} %get-tuple-element.12.es, ...), custom_call_target="tpu_custom_call" | custom-call | tf_op jit(solution)/shard_map/pallas_call | solution.py:605

commit v4 on v3

--- a/solution.py
+++ b/solution.py
@@ -95,6 +95,8 @@
     yhi = lax.div(q, ZN)
     xy = s * 2 + yhi
     half = lax.div(s, 4)
+    x = lax.div(s, 2)
+    y = lax.rem(s, 2) * 2 + yhi
 
     def to(src, feat):
         return {"device_id": (src, feat), "device_id_type": pl.DeviceIdType.MESH}
@@ -113,6 +115,13 @@
     def xy_peer(d, core=c):
         i = lax.rem(xy + d, 16)
         return to(lax.div(i, 2), (lax.rem(i, 2) * ZN + z) * 2 + core)
+
+    def x_peer(d):
+        return to(lax.rem(x + d, 4) * 2 + lax.div(y, 2), f)
+
+    def y_peer(d):
+        k = lax.rem(y + d, 4)
+        return to(x * 2 + lax.div(k, 2), (lax.rem(k, 2) * ZN + z) * 2 + c)
 
     def loop(n, fn):
         def body(d, carry):
@@ -139,32 +148,52 @@
         return n // 2 + jnp.where(lax.rem(d, 2) == 0, step, -step)
 
     def gather(buf, k, m):
-        mine = buf.at[xy, 0]
+        mine = buf.at[x, y, 0]
         for d in FAR:
-            send(mine, buf.at[xy, ZN - d], k, z_peer(d), m + GROUP_OF[ZN - d])
+            send(mine, buf.at[x, y, ZN - d], k, z_peer(d), m + GROUP_OF[ZN - d])
         loop(16, lambda d: send(mine, mine, k + 1, xy_peer(d), m + 7))
 
-        def onward(g):
+        def first(g):
             lo, hi = GROUPS[g]
-            arrived(buf.at[0, lo:hi], m + g)
-            part = buf.at[xy, lo:hi]
+            arrived(buf.at[0, 0, lo:hi], m + g)
+            part = buf.at[x, y, lo:hi]
+            for d in (2, 1, 3):
+                send(part, part, k + 3, x_peer(d) if g % 2 == 0 else y_peer(d), m + 10 + g)
+
+        def second(g):
+            lo, hi = GROUPS[g]
+            arrived(buf.at[0:3, 0, lo:hi], m + 10 + g)
+            part = buf.at[:, y, lo:hi] if g % 2 == 0 else buf.at[x, :, lo:hi]
+            for d in (2, 1, 3):
+                send(part, part, k + 4, y_peer(d) if g % 2 == 0 else x_peer(d), m + 14)
+
+        def direct(g):
+            lo, hi = GROUPS[g]
+            arrived(buf.at[0, 0, lo:hi], m + g)
+            part = buf.at[x, y, lo:hi]
             loop(16, lambda d: send(part, part, k + 1, xy_peer(d), m + 8))
 
-        onward(0)
-        onward(1)
-        arrived(buf.at[0, 0:15], m + 7)
+        first(0)
+        first(1)
+        arrived(buf.at[0, 0, 0:15], m + 7)
         for d in (2, 14, 1, 15):
-            send(buf.at[:, 0], buf.at[:, ZN - d], k + 2, z_peer(d), m + 9)
-        onward(2)
-        for g in (3, 4, 5, 6):
-            onward(g)
-        arrived(buf.at[0:15, 0:11], m + 8)
-        arrived(buf.at[:, 0:4], m + 9)
+            send(buf.at[:, :, 0], buf.at[:, :, ZN - d], k + 2, z_peer(d), m + 9)
+        first(2)
+        first(3)
+        for g in (4, 5, 6):
+            direct(g)
+        for g in (0, 1, 2, 3):
+            second(g)
+        arrived(buf.at[0:3, 0:3, 0:5], m + 8)
+        arrived(buf.at[0:3, :, 0:8], m + 14)
+        arrived(buf.at[:, :, 0:4], m + 9)
 
     def gathered(buf, k):
-        left(buf.at[0, 0:11], k)
-        left(buf.at[0:15, 0:12], k + 1)
-        left(buf.at[:, 0:4], k + 2)
+        left(buf.at[0, 0, 0:11], k)
+        left(buf.at[0:3, :, 0:5], k + 1)
+        left(buf.at[:, :, 0:4], k + 2)
+        left(buf.at[0:3, 0, 0:8], k + 3)
+        left(buf.at[0:3, :, 0:8], k + 4)
 
     fetched = []
     for k, (src, dst) in enumerate(((res_h, res_t), (gain_h, gain), (gw_h, gw), (uw_h, uw), (tok_h, tok), (eb_h, eb), (db_h, db))):
@@ -240,9 +269,14 @@
     def send_p1(d):
         k = far_first(SRC, d)
         send(sqs, sqr.at[k - 1], 1, src_peer(k, c))
-        send(gu.at[:, pl.ds(8 * lax.rem(s + k, SRC), 8)], p1r.at[k - 1], 0, src_peer(k, c))
+        send(gu.at[:, pl.ds(8 * lax.rem(s + k, SRC), 4)], p1r.at[k - 1, :, 0:4], 0, src_peer(k, c))
+
+    def send_p1_rest(d):
+        k = far_first(SRC, d)
+        send(gu.at[:, pl.ds(8 * lax.rem(s + k, SRC) + 4, 4)], p1r.at[k - 1, :, 4:8], 0, src_peer(k, c), 82)
 
     loop(SRC, send_p1)
+    loop(SRC, send_p1_rest)
 
     for k in (4, 5, 6):
         fetched[k].wait()
@@ -303,27 +337,29 @@
             fold(lambda g: rn[224 * h + 64 * g : 224 * h + 64 * g + 64], lanes)
         )
 
-    arrived(p1r, 0)
-    acts = []
-    for k in range(2):
-        acc = gu[k, pl.ds(8 * s, 8)].astype(F32)
-        for d in range(7):
-            acc = acc + p1r[d, k].astype(F32)
-        acts.append(acc * rt[pl.ds(8 * s, 8)])
-    hb[...] = (jax.nn.gelu(acts[0], approximate=True) * acts[1]).astype(BF16)
-
     slot = jnp.where(c == half, 0, 1)
-    place = hh.at[slot, pl.ds(8 * lax.rem(s, 4), 8)]
-
-    @pl.when(c == half)
-    def _():
-        pltpu.make_async_copy(hb, place, rsem.at[2]).start()
-
-    @pl.when(c != half)
-    def _():
-        send(hb, place, 2, src_peer(0, half))
-
-    loop(SRC, lambda d: send(hb, place, 2, src_peer(d, half)))
+    for n in range(2):
+        at = slice(4 * n, 4 * n + 4)
+        arrived(p1r.at[:, :, at], 82 * n)
+        acts = []
+        for k in range(2):
+            acc = gu[k, pl.ds(8 * s + 4 * n, 4)].astype(F32)
+            for d in range(7):
+                acc = acc + p1r[d, k, at].astype(F32)
+            acts.append(acc * rt[pl.ds(8 * s + 4 * n, 4)])
+        hb[at] = (jax.nn.gelu(acts[0], approximate=True) * acts[1]).astype(BF16)
+        ours = hb.at[at]
+        place = hh.at[slot, pl.ds(8 * lax.rem(s, 4) + 4 * n, 4)]
+
+        @pl.when(c == half)
+        def _():
+            pltpu.make_async_copy(ours, place, rsem.at[2]).start()
+
+        @pl.when(c != half)
+        def _():
+            send(ours, place, 2, src_peer(0, half))
+
+        loop(SRC, lambda d: send(ours, place, 2, src_peer(d, half)))
     shares[1].wait()
     arrived(hh, 2)
     acc = jnp.zeros((HALF, 384), F32)
@@ -352,12 +388,12 @@
     acc = ot[q].astype(F32)
     for d in range(31):
         acc = acc + p3r[d].astype(F32)
-    gs[xy, 0] = (rest[q] + acc).astype(BF16)
-
-    gather(gs, 4, 14)
+    gs[x, y, 0] = (rest[q] + acc).astype(BF16)
+
+    gather(gs, 17, 52)
 
     def picked(buf, first, n):
-        return jnp.concatenate([buf[t // 16, place_of[t % 16]] for t in range(first, first + n)], axis=0)
+        return jnp.concatenate([buf[t // 64, t // 16 % 4, place_of[t % 16]] for t in range(first, first + n)], axis=0)
 
     acc = jnp.zeros((HALF, 128), F32)
     rem = jnp.zeros((64, 128), F32)
@@ -421,10 +457,10 @@
             ),
         )
 
+    for k, d in enumerate((2, 14, 1, 15)):
+        send(tt.at[:, d], zb.at[k], 8, z_peer(d), 31)
     for g in (6, 4, 5):
         across(g)
-    for k, d in enumerate((2, 14, 1, 15)):
-        send(tt.at[:, d], zb.at[k], 8, z_peer(d), 31)
     for g in (2, 3, 0, 1):
         across(g)
     lat_t[...] = jnp.concatenate([latents, jnp.zeros((32, 256), F32)], axis=0).T.astype(BF16)
@@ -465,8 +501,8 @@
     row = lax.rem(t, 14)
     err = (acc + bias[col, 0:1] - ss[t].astype(F32)).astype(BF16)
     tw = twb[pl.ds(pl.multiple_of(off + 16 * row, 16), 16)]
-    ee[xy, 0] = (2.0 * tw * err.astype(F32)).astype(BF16)
-    gather(ee, 10, 34)
+    ee[x, y, 0] = (2.0 * tw * err.astype(F32)).astype(BF16)
+    gather(ee, 22, 67)
 
     def err_cols(p):
         return jnp.concatenate([picked(ee, 28 * p, 14), picked(ee, 28 * p + 14, 14)], axis=1)
@@ -514,6 +550,29 @@
         send(n7.at[0], n7z.at[k - 1], 15, z_peer(k), 50)
 
     loop(ZN, send_n)
+
+    left(p1r, 0)
+    left(sqr, 1)
+
+    @pl.when(c == half)
+    def _():
+        left(hh.at[0, 0:28], 2)
+        left(hh.at[1, 0:28], 2)
+
+    @pl.when(c != half)
+    def _():
+        left(hh, 2)
+
+    left(p3r, 3)
+    gathered(gs, 17)
+    left(p5r.at[:, 0:12], 7)
+    left(zb, 8)
+    left(p5z, 9)
+    gathered(ee, 22)
+    left(egs, 13)
+    left(dgs, 14)
+    for k in range(3, 7):
+        loads[k].wait()
     arrived(n7z, 50)
     for d in range(15):
         acc = acc + n7z[d]
@@ -529,29 +588,7 @@
     for d in range(31):
         acc = acc + n7x[d]
     clip[...] = jnp.broadcast_to(lax.rsqrt(jnp.sum(acc, keepdims=True) + 1e-12), (8, 128))
-    for k in range(3, 7):
-        loads[k].wait()
-
-    left(p1r, 0)
-    left(sqr, 1)
-
-    @pl.when(c == half)
-    def _():
-        left(hh.at[0, 0:28], 2)
-        left(hh.at[1, 0:28], 2)
-
-    @pl.when(c != half)
-    def _():
-        left(hh, 2)
-
-    left(p3r, 3)
-    gathered(gs, 4)
-    left(p5r.at[:, 0:12], 7)
-    left(zb, 8)
-    left(p5z, 9)
-    gathered(ee, 10)
-    left(egs, 13)
-    left(dgs, 14)
+
     left(n7z, 15)
     left(n7x, 16)
 
@@ -570,14 +607,14 @@
         V((7, 2, 8, 16, 128), BF16), V((8, 128), F32), V((7, 8, 128), F32), V((8, 16, 128), BF16),
         V((2, 32, 16, 128), BF16), V((2, 384, 384), BF16), V((512, 256), F32), V((32, 16, 128), F32),
         V((32, 16, 128), BF16), V((31, 16, 128), BF16),
-        V((16, 16, 16, 128), BF16), V((256, 16, 128), BF16), V((512, 128), F32), V((18, 8, 128), F32),
+        V((4, 4, 16, 16, 128), BF16), V((256, 16, 128), BF16), V((512, 128), F32), V((18, 8, 128), F32),
         V((HALF, 256), F32), V((256, 256), BF16), V((16, 16, 16, 128), BF16), V((15, 16, 16, 128), BF16),
         V((4, 16, 16, 128), BF16), V((16, 16, 128), BF16), V((16, 16, 128), BF16), V((11, 16, 128), BF16),
-        V((16, 16, 16, 128), BF16), V((D, 256), BF16),
+        V((4, 4, 16, 16, 128), BF16), V((D, 256), BF16),
         V((128, D), BF16), V((128, D), BF16), V((D, 128), BF16), V((D, 128), BF16),
         V((2, 8, 128), F32), V((15, 8, 128), F32), V((31, 8, 128), F32),
         pltpu.SemaphoreType.DMA((14,)), pltpu.SemaphoreType.DMA((4,)), pltpu.SemaphoreType.DMA((4,)),
-        pltpu.SemaphoreType.DMA((17,)), pltpu.SemaphoreType.DMA((52,)),
+        pltpu.SemaphoreType.DMA((27,)), pltpu.SemaphoreType.DMA((83,)),
     ]
     operands = [
         pltpu.with_memory_space_constraint(v, pltpu.HBM)

time: 110 us -> 108 us (0.982)
  Pallas kernels: 110 us -> 107 us
    pallas_call x1, Pallas kernels: 107 us -> 105 us  [local(): pl.pallas_call(kernel, out_shape=(jax.ShapeDtypeStruct((D, 128), F32), ja...]
where the time goes in v4:
time: 108 us
  Pallas kernels  107 us (99%)
    pallas_call x1, Pallas kernels, local(): pl.pallas_call(kernel, out_shape=(jax.ShapeDtypeStruct((D, 128), F32), ja...  105 us
    pallas_call x1, Pallas kernels, local(): pl.pallas_call(adam_kernel, out_shape=(tall, flat), in_specs=[vm] * 7, ou...  2.56 us

profile of v4, /device:TPU:1, one launch (start us, length us, event | category | flops | bytes accessed | tf_op | source)
XLA Modules:
  0.0 107.9 jit_solution(2721498684182578105)
XLA Ops:
  0.6 104.7 %shard_map.149 = (f32[2304,128]{1,0:T(8,128)S(1)}, f32[128,2304]{1,0:T(8,128)S(1)}, f32[8,128]{1,0:T(8,128)S(1)}, bf16[2304,128]{1,0:T(8,128)(2,1)S(1)}, bf16[23...) custom-call(bf16[288,448]{1,0:T(8,128)(2,1)} %bitcast.3, s32[1,448]{1,0:T(1,128)} %bitcast.4, ...), custom_call_target="tpu_custom_call" | custom-call | tf_op jit(solution)/shard_map/pallas_call | solution.py:627
  105.3 2.6 %shard_map.150 = (bf16[2304,128]{1,0:T(8,128)(2,1)}, bf16[128,2304]{1,0:T(8,128)(2,1)}) custom-call(f32[8,128]{1,0:T(8,128)S(1)} %get-tuple-element.9.clip, f32[2304,128]{1,0:T(8,128)S(1)} %get-tuple-element.10.eg, bf16[2304,128]{1,0:T(8,128)(2,1)S(1)} %get-tuple-element.11.ef, bf16[2304,128]{1,0:T(8,128)(2,1)S(1)} %get-tuple-element.12.es, ...), custom_call_target="tpu_custom_call" | custom-call | tf_op jit(solution)/shard_map/pallas_call | solution.py:642

commit v5 on v4

--- a/solution.py
+++ b/solution.py
@@ -112,8 +112,11 @@
     def z_peer(d):
         return to(s, (yhi * ZN + lax.rem(z + d, ZN)) * 2 + c)
 
+    def xy_index(d):
+        return lax.rem(x + lax.div(d, 4), 4) * 4 + lax.rem(y + lax.rem(d, 4), 4)
+
     def xy_peer(d, core=c):
-        i = lax.rem(xy + d, 16)
+        i = xy_index(d)
         return to(lax.div(i, 2), (lax.rem(i, 2) * ZN + z) * 2 + core)
 
     def x_peer(d):
@@ -130,6 +133,9 @@
 
         lax.fori_loop(1, n, body, 0)
 
+    def loop_xy(fn):
+        loop(16, lambda d: fn(lax.rem(26 - d, 15) + 1))
+
     def send(src, dst, k, where, at=None):
         pltpu.make_async_remote_copy(
             src_ref=src, dst_ref=dst, send_sem=ssem.at[k], recv_sem=rsem.at[k if at is None else at], **where
@@ -151,7 +157,7 @@
         mine = buf.at[x, y, 0]
         for d in FAR:
             send(mine, buf.at[x, y, ZN - d], k, z_peer(d), m + GROUP_OF[ZN - d])
-        loop(16, lambda d: send(mine, mine, k + 1, xy_peer(d), m + 7))
+        loop_xy(lambda d: send(mine, mine, k + 1, xy_peer(d), m + 7))
 
         def first(g):
             lo, hi = GROUPS[g]
@@ -171,7 +177,7 @@
             lo, hi = GROUPS[g]
             arrived(buf.at[0, 0, lo:hi], m + g)
             part = buf.at[x, y, lo:hi]
-            loop(16, lambda d: send(part, part, k + 1, xy_peer(d), m + 8))
+            loop_xy(lambda d: send(part, part, k + 1, xy_peer(d), m + 8))
 
         first(0)
         first(1)
@@ -450,10 +456,9 @@
 
     def across(g):
         lo, hi = GROUPS[g]
-        loop(
-            16,
+        loop_xy(
             lambda d: send(
-                tt.at[lax.rem(xy + d, 16), lo:hi], p5r.at[d - 1, lo:hi], 7, xy_peer(d), 24 + g
+                tt.at[xy_index(d), lo:hi], p5r.at[d - 1, lo:hi], 7, xy_peer(d), 24 + g
             ),
         )
 
@@ -486,7 +491,7 @@
         for d in range(4):
             acc = acc + zb[d, k].astype(F32)
         own[k] = acc.astype(BF16)
-    loop(16, lambda d: send(own.at[lax.rem(xy + d, 16)], p5r.at[d - 1, 0], 7, xy_peer(d), 32))
+    loop_xy(lambda d: send(own.at[xy_index(d)], p5r.at[d - 1, 0], 7, xy_peer(d), 32))
     for g in (2, 3, 0, 1):
         onward(g)
     arrived(p5r.at[:, 0], 32)
@@ -582,7 +587,7 @@
         send(n7.at[1], n7x.at[d - 1], 16, xy_peer(d), 51)
         send(n7.at[1], n7x.at[d + 15], 16, xy_peer(d, 1 - c), 51)
 
-    loop(16, send_xy)
+    loop_xy(send_xy)
     send(n7.at[1], n7x.at[15], 16, other, 51)
     arrived(n7x, 51)
     for d in range(31):

time: 108 us -> 107 us (level)
  no operation moved by 1% of the time
where the time goes in v5:
time: 107 us
  Pallas kernels  106 us (99%)
    pallas_call x1, Pallas kernels, local(): pl.pallas_call(kernel, out_shape=(jax.ShapeDtypeStruct((D, 128), F32), ja...  104 us
    pallas_call x1, Pallas kernels, local(): pl.pallas_call(adam_kernel, out_shape=(tall, flat), in_specs=[vm] * 7, ou...  2.56 us

profile of v5, /device:TPU:1, one launch (start us, length us, event | category | flops | bytes accessed | tf_op | source)
XLA Modules:
  0.0 107.1 jit_solution(4527053403690424304)
XLA Ops:
  0.6 103.9 %shard_map.149 = (f32[2304,128]{1,0:T(8,128)S(1)}, f32[128,2304]{1,0:T(8,128)S(1)}, f32[8,128]{1,0:T(8,128)S(1)}, bf16[2304,128]{1,0:T(8,128)(2,1)S(1)}, bf16[23...) custom-call(bf16[288,448]{1,0:T(8,128)(2,1)} %bitcast.3, s32[1,448]{1,0:T(1,128)} %bitcast.4, ...), custom_call_target="tpu_custom_call" | custom-call | tf_op jit(solution)/shard_map/pallas_call | solution.py:632
  104.5 2.6 %shard_map.150 = (bf16[2304,128]{1,0:T(8,128)(2,1)}, bf16[128,2304]{1,0:T(8,128)(2,1)}) custom-call(f32[8,128]{1,0:T(8,128)S(1)} %get-tuple-element.9.clip, f32[2304,128]{1,0:T(8,128)S(1)} %get-tuple-element.10.eg, bf16[2304,128]{1,0:T(8,128)(2,1)S(1)} %get-tuple-element.11.ef, bf16[2304,128]{1,0:T(8,128)(2,1)S(1)} %get-tuple-element.12.es, ...), custom_call_target="tpu_custom_call" | custom-call | tf_op jit(solution)/shard_map/pallas_call | solution.py:647
